TPU v7x, 1024 devices: a whole 4x8x16 slice. The times are simulated.
1024 devices in a mesh: gx: 32 (over x_lo, y, core), gy: 32 (over x_hi, z).
Axes of the slice: x: 4 (x_hi: 2, x_lo: 2; x = x_hi * 2 + x_lo), y: 8, z: 16, core: 2. Of those that a mesh axis runs over, the one named last changes fastest.
Arguments:
- velocity: float32 [3, 512, 512, 128], P(None, 'gx', 'gy'), may hold values from -6 to 6
- stress: float32 [6, 512, 512, 128], P(None, 'gx', 'gy'), may hold values from -6 to 6
- buoyancy: float32 [512, 512, 128], P('gx', 'gy'), may hold values from 0.5 to 2
- lame_lambda: float32 [512, 512, 128], P('gx', 'gy'), may hold values from 0.5 to 2
- shear_modulus: float32 [512, 512, 128], P('gx', 'gy'), may hold values from 0.5 to 2
- slot_moment: float32 [32, 32, 6, 64], P('gx', 'gy'), may hold values from -24 to 24
- slot_signal: float32 [32, 32, 64], P('gx', 'gy'), may hold values from 0.5 to 2
- slot_x: int32 [32, 32, 64], P('gx', 'gy'), may hold values from 0 to 15
- slot_y: int32 [32, 32, 64], P('gx', 'gy'), may hold values from 0 to 15
- slot_z: int32 [32, 32, 64], P('gx', 'gy'), may hold values from 0 to 127
- slot_count: int32 [32, 32, 1], P('gx', 'gy'), may hold values from 0 to 64, as said below
Outputs:
- new_velocity: float32 [3, 512, 512, 128], P(None, 'gx', 'gy')
- new_stress: float32 [6, 512, 512, 128], P(None, 'gx', 'gy')
Inputs may be any that keep to these rules, and one draw needn't show every extreme that they name: `slot_count`: slots at or beyond a tile's count are unused; at least one tile uses all 64 slots.
All inputs are finite; a program needn't handle non-finite values.
Results may differ from a plain program's by a relative error of at most 0.00005.
Values sent between devices are 32-bit elements; how exact they have to be, the bound alone decides.
A program may use at most 64 MiB of HBM per device.

v0:
```python
import jax
import jax.numpy as jnp
from jax import lax
from jax.sharding import PartitionSpec as P

coef_one = 9.0 / 8.0
coef_two = -1.0 / 24.0
time_step = 0.1
pairs = ((0, 3, 4), (3, 1, 5), (4, 5, 2))
deriv_table = (1.0 / 24.0, -9.0 / 8.0, 9.0 / 8.0, -1.0 / 24.0)
weight_table = (-1.0 / 16.0, 9.0 / 16.0, 9.0 / 16.0, -1.0 / 16.0)


def with_halo(cells, sides, width):
    for axis, dim in sides:
        count = lax.axis_size(axis)
        ends = count - 1
        head = lax.slice_in_dim(cells, 0, width, axis=dim)
        tail = lax.slice_in_dim(cells, cells.shape[dim] - width, cells.shape[dim], axis=dim)
        cells = jnp.concatenate(
            [
                lax.ppermute(tail, axis, [(i, (i + 1) % count) for i in range(ends)]),
                cells,
                lax.ppermute(head, axis, [((i + 1) % count, i) for i in range(ends)]),
            ],
            axis=dim,
        )
    return cells


def derive(padded, axis, forward):
    count = padded.shape[axis] - 4

    def part(low):
        return lax.slice_in_dim(padded, low, low + count, axis=axis)

    if forward:
        value = coef_one * (part(3) - part(2)) + coef_two * (part(4) - part(1))
    else:
        value = coef_one * (part(2) - part(1)) + coef_two * (part(3) - part(0))
    for other in range(3):
        if other != axis:
            value = lax.slice_in_dim(value, 2, value.shape[other] - 2, axis=other)
    return value


def velocity_step(velocity, padded_stress, buoyancy, force):
    sxx, syy, szz, sxy, sxz, syz = [padded_stress[k] for k in range(6)]
    accel_x = derive(sxx, 0, True) + derive(sxy, 1, False) + derive(sxz, 2, False)
    accel_y = derive(sxy, 0, False) + derive(syy, 1, True) + derive(syz, 2, False)
    accel_z = derive(sxz, 0, False) + derive(syz, 1, False) + derive(szz, 2, True)
    accel = jnp.stack([accel_x, accel_y, accel_z])
    return velocity + time_step * buoyancy[None] * (accel + force)


def stress_step(stress, padded_vel, lame_lambda, shear_modulus):
    vel_x, vel_y, vel_z = (padded_vel[0], padded_vel[1], padded_vel[2])
    exx = derive(vel_x, 0, False)
    eyy = derive(vel_y, 1, False)
    ezz = derive(vel_z, 2, False)
    trace = exx + eyy + ezz
    sxx = stress[0] + time_step * (lame_lambda * trace + 2.0 * shear_modulus * exx)
    syy = stress[1] + time_step * (lame_lambda * trace + 2.0 * shear_modulus * eyy)
    szz = stress[2] + time_step * (lame_lambda * trace + 2.0 * shear_modulus * ezz)
    sxy = stress[3] + time_step * shear_modulus * (derive(vel_x, 1, True) + derive(vel_y, 0, True))
    sxz = stress[4] + time_step * shear_modulus * (derive(vel_x, 2, True) + derive(vel_z, 0, True))
    syz = stress[5] + time_step * shear_modulus * (derive(vel_y, 2, True) + derive(vel_z, 1, True))
    return jnp.stack([sxx, syy, szz, sxy, sxz, syz])


def factor(position, length, table):
    offset = jnp.arange(length, dtype=jnp.int32)[None, :] - position[:, None] - 1
    total = jnp.zeros(offset.shape, jnp.float32)
    for k in range(4):
        total = total + table[k] * (offset == k).astype(jnp.float32)
    return total


def inner(array, axis):
    return lax.slice_in_dim(array, 2, array.shape[axis] - 2, axis=axis)


def rim_pair(array, axis):
    size = array.shape[axis]
    low = lax.slice_in_dim(array, 0, 2, axis=axis)
    high = lax.slice_in_dim(array, size - 2, size, axis=axis)
    middle_shape = list(array.shape)
    middle_shape[axis] = size - 8
    middle = jnp.zeros(tuple(middle_shape), array.dtype)
    return jnp.concatenate([low, middle, high], axis=axis)


def pad_depth(array):
    return jnp.pad(array, ((0, 0), (0, 0), (0, 0), (2, 2)))


def amplitudes(moment, scaled):
    return jnp.stack(
        [jnp.stack([-moment[pairs[i][j]] * scaled for j in range(3)], -1) for i in range(3)], -2
    )


def spread_sources(amp, pos_x, pos_y, pos_z, cells_x, cells_y, depth):
    count = amp.shape[0]
    xw = factor(pos_x, cells_x + 4, weight_table)
    xd = factor(pos_x, cells_x + 4, deriv_table)
    yw = factor(pos_y, cells_y + 4, weight_table)
    yd = factor(pos_y, cells_y + 4, deriv_table)
    zw = factor(pos_z, depth + 4, weight_table)
    zd = factor(pos_z, depth + 4, deriv_table)
    along_x = (xd, xw, xw)
    along_y = (yw, yd, yw)
    along_z = (zw, zw, zd)
    left = jnp.concatenate(
        [jnp.einsum("si,sa,sb->iabs", amp[:, :, j], along_x[j], along_y[j]) for j in range(3)],
        axis=3,
    )
    right = jnp.concatenate(list(along_z), axis=0)
    spread = jnp.dot(
        left.reshape(-1, 3 * count),
        right,
        precision=lax.Precision.HIGHEST,
        preferred_element_type=jnp.float32,
    )
    return spread.reshape(3, cells_x + 4, cells_y + 4, depth + 4)[:, :, :, 2 : depth + 2]


def local(
    velocity,
    stress,
    buoyancy,
    lame_lambda,
    shear_modulus,
    slot_moment,
    slot_signal,
    slot_x,
    slot_y,
    slot_z,
    slot_count,
):
    cells_x = velocity.shape[1]
    cells_y = velocity.shape[2]
    depth = velocity.shape[3]
    slots = slot_signal.shape[2]
    live = (jnp.arange(slots, dtype=jnp.int32) < slot_count[0, 0, 0]).astype(jnp.float32)
    scaled = slot_signal[0, 0] * live
    amp = amplitudes(slot_moment[0, 0], scaled)
    spread = spread_sources(amp, slot_x[0, 0], slot_y[0, 0], slot_z[0, 0], cells_x, cells_y, depth)
    padded_stress = with_halo(stress, (("gx", 1), ("gy", 2)), 2)
    sent_rows = rim_pair(spread, 1)
    got_rows = with_halo(sent_rows, (("gx", 1),), 2)
    partial_value = inner(spread, 1) + rim_pair(got_rows, 1)
    sent_columns = rim_pair(partial_value, 2)
    got_columns = with_halo(sent_columns, (("gy", 2),), 2)
    force = inner(partial_value, 2) + rim_pair(got_columns, 2)
    new_velocity = velocity_step(velocity, pad_depth(padded_stress), buoyancy, force)
    padded_vel = with_halo(new_velocity, (("gx", 1), ("gy", 2)), 2)
    new_stress = stress_step(stress, pad_depth(padded_vel), lame_lambda, shear_modulus)
    return (new_velocity, new_stress)


def solution(mesh):
    in_specs = (
        P(None, "gx", "gy", None),
        P(None, "gx", "gy", None),
        P("gx", "gy", None),
        P("gx", "gy", None),
        P("gx", "gy", None),
        P("gx", "gy", None, None),
        P("gx", "gy", None),
        P("gx", "gy", None),
        P("gx", "gy", None),
        P("gx", "gy", None),
        P("gx", "gy", None),
    )
    out_specs = (P(None, "gx", "gy", None), P(None, "gx", "gy", None))
    return jax.shard_map(local, mesh=mesh, in_specs=in_specs, out_specs=out_specs, check_vma=False)
```

profile of v0, /device:TPU:6, one launch (start us, length us, event | category | flops | bytes accessed | tf_op | source)
XLA Modules:
  0.0 85.4 jit_solution(4385257828373739920)
XLA Ops:
  0.6 1.0 %fusion.114 = (f32[6,2,16,128]{3,2,1,0:T(8,128)S(1)}, f32[6,2,16,128]{3,2,1,0:T(8,128)S(1)}) fusion(f32[6,16,16,128]{3,2,1,0:T(8,128)} %param.12), kind=kLoop, calls=%fused_computation.217 | loop fusion | bytes 393216 | tf_op jit(solution)/shard_map/slice | solution.py:18
  1.6 5.1 %collective-permute-start.1 = (f32[6,2,16,128]{3,2,1,0:T(8,128)S(1)}, f32[6,2,16,128]{3,2,1,0:T(8,128)S(1)}, u32[]{:S(2)}, u32[]{:S(2)}) collective-permute-start(f32[6,2,16,128]{3,2,1,0:T(8,128)S(1)} %get-tuple-element.26), channel_id=1, source_target_pairs={{32,0},{64,32},{96,64},{128,96},{160,128},{192,160},{224,192},{256... | collective-permute-start | bytes 294920 | tf_op jit(solution)/shard_map/ppermute | solution.py:24
  6.7 1.9 %collective-permute-start = (f32[6,2,16,128]{3,2,1,0:T(8,128)S(1)}, f32[6,2,16,128]{3,2,1,0:T(8,128)S(1)}, u32[]{:S(2)}, u32[]{:S(2)}) collective-permute-start(f32[6,2,16,128]{3,2,1,0:T(8,128)S(1)} %get-tuple-element.27), channel_id=1, source_target_pairs={{0,32},{32,64},{64,96},{96,128},{128,160},{160,192},{192,224},{224... | collective-permute-start | bytes 294920 | tf_op jit(solution)/shard_map/ppermute | solution.py:22
  9.3 0.7 bitcast_multiply_fusion.5
  9.9 0.7 bitcast_multiply_fusion.4
  10.7 0.7 select_add_fusion.5
  11.4 0.7 select_add_fusion.2
  12.1 0.7 select_add_fusion.1
  13.1 1.5 %fusion.1 = f32[3,20,20,132]{3,2,1,0:T(8,128)S(1)} fusion(f32[3,20,20,64]{3,2,1,0:T(8,128)S(1)} %get-tuple-element.83, f32[3,20,20,64]{3,2,1,0:T(8,128)S(1)} %get-tuple-element.103, f32[3,20,20,64]{3,2,1,0:T(8,128)S(1)} %get-tuple-element.82, f32[64,132]{0,1:T(8,128)S(1)} %get-tuple-element.95, f32[64,132]{0,1:T(8,128)S(1)} %get-tuple-element.94), kind=kOutput, calls=%fused_computation.11 | convolution fusion | flops 365465088 | bytes 1622784 | tf_op jit(solution)/shard_map/dot_general | solution.py:119
  14.6 2.1 %collective-permute-start.4 = (f32[3,2,20,128]{3,2,1,0:T(8,128)S(1)}, f32[3,2,20,128]{3,2,1,0:T(8,128)S(1)}, u32[]{:S(2)}, u32[]{:S(2)}) collective-permute-start(f32[3,2,20,128]{3,2,1,0:T(8,128)S(1)} %get-tuple-element.22), channel_id=1, source_target_pairs={{0,32},{32,64},{64,96},{96,128},{128,160},{160,192},{192,224},{224... | collective-permute-start | bytes 184328 | tf_op jit(solution)/shard_map/ppermute | solution.py:22
  16.7 5.8 %collective-permute-start.5 = (f32[3,2,20,128]{3,2,1,0:T(8,128)S(1)}, f32[3,2,20,128]{3,2,1,0:T(8,128)S(1)}, u32[]{:S(2)}, u32[]{:S(2)}) collective-permute-start(f32[3,2,20,128]{3,2,1,0:T(8,128)S(1)} %get-tuple-element.23), channel_id=1, source_target_pairs={{32,0},{64,32},{96,64},{128,96},{160,128},{192,160},{224,192},{256... | collective-permute-start | bytes 184328 | tf_op jit(solution)/shard_map/ppermute | solution.py:24
  22.6 1.8 %collective-permute-done.5 = f32[3,2,20,128]{3,2,1,0:T(8,128)S(1)} collective-permute-done((f32[3,2,20,128]{3,2,1,0:T(8,128)S(1)}, f32[3,2,20,128]{3,2,1,0:T(8,128)S(1)}, u32[]{:S(2)}, u32[]{:S(2)}) %collective-permute-start.5) | collective-permute-done | bytes 61472 | tf_op jit(solution)/shard_map/ppermute | solution.py:24
  24.9 4.3 %collective-permute-start.2 = (f32[6,20,2,128]{3,2,1,0:T(2,128)S(1)}, f32[6,20,2,128]{3,2,1,0:T(2,128)S(1)}, u32[]{:S(2)}, u32[]{:S(2)}) collective-permute-start(f32[6,20,2,128]{3,2,1,0:T(2,128)S(1)} %get-tuple-element.24), channel_id=1, source_target_pairs={{0,1},{1,2},{2,3},{3,4},{4,5},{5,6},{6,7},{7,8},{8,9},{9,10},{10,1... | collective-permute-start | bytes 368648 | tf_op jit(solution)/shard_map/ppermute | solution.py:22
  29.2 16.4 %collective-permute-start.3 = (f32[6,20,2,128]{3,2,1,0:T(2,128)S(1)}, f32[6,20,2,128]{3,2,1,0:T(2,128)S(1)}, u32[]{:S(2)}, u32[]{:S(2)}) collective-permute-start(f32[6,20,2,128]{3,2,1,0:T(2,128)S(1)} %get-tuple-element.25), channel_id=1, source_target_pairs={{1,0},{2,1},{3,2},{4,3},{5,4},{6,5},{7,6},{8,7},{9,8},{10,9},{11,1... | collective-permute-start | bytes 368648 | tf_op jit(solution)/shard_map/ppermute | solution.py:24
  45.6 1.9 %collective-permute-start.6 = (f32[3,16,2,128]{3,2,1,0:T(2,128)S(1)}, f32[3,16,2,128]{3,2,1,0:T(2,128)S(1)}, u32[]{:S(2)}, u32[]{:S(2)}) collective-permute-start(f32[3,16,2,128]{3,2,1,0:T(2,128)S(1)} %get-tuple-element.28), channel_id=1, source_target_pairs={{0,1},{1,2},{2,3},{3,4},{4,5},{5,6},{6,7},{7,8},{8,9},{9,10},{10,1... | collective-permute-start | bytes 147464 | tf_op jit(solution)/shard_map/ppermute | solution.py:22
  47.6 7.5 %collective-permute-start.7 = (f32[3,16,2,128]{3,2,1,0:T(2,128)S(1)}, f32[3,16,2,128]{3,2,1,0:T(2,128)S(1)}, u32[]{:S(2)}, u32[]{:S(2)}) collective-permute-start(f32[3,16,2,128]{3,2,1,0:T(2,128)S(1)} %get-tuple-element.29), channel_id=1, source_target_pairs={{1,0},{2,1},{3,2},{4,3},{5,4},{6,5},{7,6},{8,7},{9,8},{10,9},{11,1... | collective-permute-start | bytes 147464 | tf_op jit(solution)/shard_map/ppermute | solution.py:24
  55.1 1.3 %select_maximum_fusion = f32[6,20,20,132]{3,2,1,0:T(8,128)S(1)} fusion(f32[6,20,2,128]{3,2,1,0:T(2,128)S(1)} %collective-permute-done.3, f32[6,20,16,128]{3,2,1,0:T(8,128)S(1)} %constant_dynamic-update-slice_fusion, f32[6,20,2,128]{3,2,1,0:T(2,128)S(1)} %collective-permute-done.2), kind=kLoop, calls=%fused_computation.2 | loop fusion | flops 2534400 | bytes 2496000 | tf_op jit(solution)/shard_map/concatenate | solution.py:20
  56.9 0.3 fusion.127
  57.4 0.5 fusion.123
  58.9 0.4 copy-done.3
  59.5 1.9 %collective-permute-start.8 = (f32[3,2,16,128]{3,2,1,0:T(8,128)S(1)}, f32[3,2,16,128]{3,2,1,0:T(8,128)S(1)}, u32[]{:S(2)}, u32[]{:S(2)}) collective-permute-start(f32[3,2,16,128]{3,2,1,0:T(8,128)S(1)} %get-tuple-element.80), channel_id=1, source_target_pairs={{0,32},{32,64},{64,96},{96,128},{128,160},{160,192},{192,224},{224... | collective-permute-start | bytes 147464 | tf_op jit(solution)/shard_map/ppermute | solution.py:22
  61.5 5.8 %collective-permute-start.9 = (f32[3,2,16,128]{3,2,1,0:T(8,128)S(1)}, f32[3,2,16,128]{3,2,1,0:T(8,128)S(1)}, u32[]{:S(2)}, u32[]{:S(2)}) collective-permute-start(f32[3,2,16,128]{3,2,1,0:T(8,128)S(1)} %get-tuple-element.81), channel_id=1, source_target_pairs={{32,0},{64,32},{96,64},{128,96},{160,128},{192,160},{224,192},{256... | collective-permute-start | bytes 147464 | tf_op jit(solution)/shard_map/ppermute | solution.py:24
  67.2 1.7 %collective-permute-done.9 = f32[3,2,16,128]{3,2,1,0:T(8,128)S(1)} collective-permute-done((f32[3,2,16,128]{3,2,1,0:T(8,128)S(1)}, f32[3,2,16,128]{3,2,1,0:T(8,128)S(1)}, u32[]{:S(2)}, u32[]{:S(2)}) %collective-permute-start.9) | collective-permute-done | bytes 49184 | tf_op jit(solution)/shard_map/ppermute | solution.py:24
  69.0 1.9 %collective-permute-start.10 = (f32[3,20,2,128]{3,2,1,0:T(2,128)S(1)}, f32[3,20,2,128]{3,2,1,0:T(2,128)S(1)}, u32[]{:S(2)}, u32[]{:S(2)}) collective-permute-start(f32[3,20,2,128]{3,2,1,0:T(2,128)S(1)} %get-tuple-element.54), channel_id=1, source_target_pairs={{0,1},{1,2},{2,3},{3,4},{4,5},{5,6},{6,7},{7,8},{8,9},{9,10},{10,1... | collective-permute-start | bytes 184328 | tf_op jit(solution)/shard_map/ppermute | solution.py:22
  70.9 7.5 %collective-permute-start.11 = (f32[3,20,2,128]{3,2,1,0:T(2,128)S(1)}, f32[3,20,2,128]{3,2,1,0:T(2,128)S(1)}, u32[]{:S(2)}, u32[]{:S(2)}) collective-permute-start(f32[3,20,2,128]{3,2,1,0:T(2,128)S(1)} %get-tuple-element.55), channel_id=1, source_target_pairs={{1,0},{2,1},{3,2},{4,3},{5,4},{6,5},{7,6},{8,7},{9,8},{10,9},{11,1... | collective-permute-start | bytes 184328 | tf_op jit(solution)/shard_map/ppermute | solution.py:24
  78.7 1.6 %collective-permute-done.11 = f32[3,20,2,128]{3,2,1,0:T(2,128)S(1)} collective-permute-done((f32[3,20,2,128]{3,2,1,0:T(2,128)S(1)}, f32[3,20,2,128]{3,2,1,0:T(2,128)S(1)}, u32[]{:S(2)}, u32[]{:S(2)}) %collective-permute-start.11) | collective-permute-done | bytes 61472 | tf_op jit(solution)/shard_map/ppermute | solution.py:24
  80.3 0.7 select_maximum_fusion.2
  81.3 0.3 fusion.118
  81.8 0.3 fusion.116
  82.7 0.7 copy-done
  83.5 0.3 bitcast_dynamic-update-slice_fusion.2
  84.5 0.9 %copy-done.6 = f32[6,16,16,128]{3,2,1,0:T(8,128)} copy-done((f32[6,16,16,128]{3,2,1,0:T(8,128)}, f32[6,16,16,128]{3,2,1,0:T(8,128)S(1)}, u32[]{:S(2)}) %copy-start.6) | copy-done | bytes 786456
  (59 shorter events, 4.7 us)
Async XLA Ops:
  1.6 23.2 %collective-permute-start.1 = (f32[6,2,16,128]{3,2,1,0:T(8,128)S(1)}, f32[6,2,16,128]{3,2,1,0:T(8,128)S(1)}, u32[]{:S(2)}, u32[]{:S(2)}) collective-permute-start(f32[6,2,16,128]{3,2,1,0:T(8,128)S(1)} %get-tuple-element.26), channel_id=1, source_target_pairs={{32,0},{64,32},{96,64},{128,96},{160,128},{192,160},{224,192},{256... | collective-permute-start | bytes 294920 | tf_op jit(solution)/shard_map/ppermute | solution.py:24
  6.7 18.0 %collective-permute-start = (f32[6,2,16,128]{3,2,1,0:T(8,128)S(1)}, f32[6,2,16,128]{3,2,1,0:T(8,128)S(1)}, u32[]{:S(2)}, u32[]{:S(2)}) collective-permute-start(f32[6,2,16,128]{3,2,1,0:T(8,128)S(1)} %get-tuple-element.27), channel_id=1, source_target_pairs={{0,32},{32,64},{64,96},{96,128},{128,160},{160,192},{192,224},{224... | collective-permute-start | bytes 294920 | tf_op jit(solution)/shard_map/ppermute | solution.py:22
  13.1 9.4 %copy-start.5 = (f32[16,16,128]{2,1,0:T(8,128)S(1)}, f32[16,16,128]{2,1,0:T(8,128)}, u32[]{:S(2)}) copy-start(f32[16,16,128]{2,1,0:T(8,128)} %param.13) | copy-start | bytes 393220
  14.5 10.2 %copy-start.2 = (f32[6,16,16,128]{3,2,1,0:T(8,128)S(1)}, f32[6,16,16,128]{3,2,1,0:T(8,128)}, u32[]{:S(2)}) copy-start(f32[6,16,16,128]{3,2,1,0:T(8,128)} %param.12) | copy-start | bytes 2359300
  14.6 7.9 %collective-permute-start.4 = (f32[3,2,20,128]{3,2,1,0:T(8,128)S(1)}, f32[3,2,20,128]{3,2,1,0:T(8,128)S(1)}, u32[]{:S(2)}, u32[]{:S(2)}) collective-permute-start(f32[3,2,20,128]{3,2,1,0:T(8,128)S(1)} %get-tuple-element.22), channel_id=1, source_target_pairs={{0,32},{32,64},{64,96},{96,128},{128,160},{160,192},{192,224},{224... | collective-permute-start | bytes 184328 | tf_op jit(solution)/shard_map/ppermute | solution.py:22
  16.7 7.7 %collective-permute-start.5 = (f32[3,2,20,128]{3,2,1,0:T(8,128)S(1)}, f32[3,2,20,128]{3,2,1,0:T(8,128)S(1)}, u32[]{:S(2)}, u32[]{:S(2)}) collective-permute-start(f32[3,2,20,128]{3,2,1,0:T(8,128)S(1)} %get-tuple-element.23), channel_id=1, source_target_pairs={{32,0},{64,32},{96,64},{128,96},{160,128},{192,160},{224,192},{256... | collective-permute-start | bytes 184328 | tf_op jit(solution)/shard_map/ppermute | solution.py:24
  24.9 30.2 %collective-permute-start.2 = (f32[6,20,2,128]{3,2,1,0:T(2,128)S(1)}, f32[6,20,2,128]{3,2,1,0:T(2,128)S(1)}, u32[]{:S(2)}, u32[]{:S(2)}) collective-permute-start(f32[6,20,2,128]{3,2,1,0:T(2,128)S(1)} %get-tuple-element.24), channel_id=1, source_target_pairs={{0,1},{1,2},{2,3},{3,4},{4,5},{5,6},{6,7},{7,8},{8,9},{9,10},{10,1... | collective-permute-start | bytes 368648 | tf_op jit(solution)/shard_map/ppermute | solution.py:22
  29.2 25.9 %collective-permute-start.3 = (f32[6,20,2,128]{3,2,1,0:T(2,128)S(1)}, f32[6,20,2,128]{3,2,1,0:T(2,128)S(1)}, u32[]{:S(2)}, u32[]{:S(2)}) collective-permute-start(f32[6,20,2,128]{3,2,1,0:T(2,128)S(1)} %get-tuple-element.25), channel_id=1, source_target_pairs={{1,0},{2,1},{3,2},{4,3},{5,4},{6,5},{7,6},{8,7},{9,8},{10,9},{11,1... | collective-permute-start | bytes 368648 | tf_op jit(solution)/shard_map/ppermute | solution.py:24
  45.6 13.2 %collective-permute-start.6 = (f32[3,16,2,128]{3,2,1,0:T(2,128)S(1)}, f32[3,16,2,128]{3,2,1,0:T(2,128)S(1)}, u32[]{:S(2)}, u32[]{:S(2)}) collective-permute-start(f32[3,16,2,128]{3,2,1,0:T(2,128)S(1)} %get-tuple-element.28), channel_id=1, source_target_pairs={{0,1},{1,2},{2,3},{3,4},{4,5},{5,6},{6,7},{7,8},{8,9},{9,10},{10,1... | collective-permute-start | bytes 147464 | tf_op jit(solution)/shard_map/ppermute | solution.py:22
  47.6 11.3 %collective-permute-start.7 = (f32[3,16,2,128]{3,2,1,0:T(2,128)S(1)}, f32[3,16,2,128]{3,2,1,0:T(2,128)S(1)}, u32[]{:S(2)}, u32[]{:S(2)}) collective-permute-start(f32[3,16,2,128]{3,2,1,0:T(2,128)S(1)} %get-tuple-element.29), channel_id=1, source_target_pairs={{1,0},{2,1},{3,2},{4,3},{5,4},{6,5},{7,6},{8,7},{9,8},{10,9},{11,1... | collective-permute-start | bytes 147464 | tf_op jit(solution)/shard_map/ppermute | solution.py:24
  58.3 1.0 %copy-start.3 = (f32[3,16,16,128]{3,2,1,0:T(8,128)S(1)}, f32[3,16,16,128]{3,2,1,0:T(8,128)}, u32[]{:S(2)}) copy-start(f32[3,16,16,128]{3,2,1,0:T(8,128)} %param.11) | copy-start | bytes 1179652
  59.5 21.7 %copy-start.1 = (f32[3,16,16,128]{3,2,1,0:T(8,128)}, f32[3,16,16,128]{3,2,1,0:T(8,128)S(1)}, u32[]{:S(2)}) copy-start(f32[3,16,16,128]{3,2,1,0:T(8,128)S(1)} %fusion.22) | copy-start | bytes 1179652
  59.5 7.7 %collective-permute-start.8 = (f32[3,2,16,128]{3,2,1,0:T(8,128)S(1)}, f32[3,2,16,128]{3,2,1,0:T(8,128)S(1)}, u32[]{:S(2)}, u32[]{:S(2)}) collective-permute-start(f32[3,2,16,128]{3,2,1,0:T(8,128)S(1)} %get-tuple-element.80), channel_id=1, source_target_pairs={{0,32},{32,64},{64,96},{96,128},{128,160},{160,192},{192,224},{224... | collective-permute-start | bytes 147464 | tf_op jit(solution)/shard_map/ppermute | solution.py:22
  61.5 7.5 %collective-permute-start.9 = (f32[3,2,16,128]{3,2,1,0:T(8,128)S(1)}, f32[3,2,16,128]{3,2,1,0:T(8,128)S(1)}, u32[]{:S(2)}, u32[]{:S(2)}) collective-permute-start(f32[3,2,16,128]{3,2,1,0:T(8,128)S(1)} %get-tuple-element.81), channel_id=1, source_target_pairs={{32,0},{64,32},{96,64},{128,96},{160,128},{192,160},{224,192},{256... | collective-permute-start | bytes 147464 | tf_op jit(solution)/shard_map/ppermute | solution.py:24
  69.0 9.7 %collective-permute-start.10 = (f32[3,20,2,128]{3,2,1,0:T(2,128)S(1)}, f32[3,20,2,128]{3,2,1,0:T(2,128)S(1)}, u32[]{:S(2)}, u32[]{:S(2)}) collective-permute-start(f32[3,20,2,128]{3,2,1,0:T(2,128)S(1)} %get-tuple-element.54), channel_id=1, source_target_pairs={{0,1},{1,2},{2,3},{3,4},{4,5},{5,6},{6,7},{7,8},{8,9},{9,10},{10,1... | collective-permute-start | bytes 184328 | tf_op jit(solution)/shard_map/ppermute | solution.py:22
  70.9 9.4 %collective-permute-start.11 = (f32[3,20,2,128]{3,2,1,0:T(2,128)S(1)}, f32[3,20,2,128]{3,2,1,0:T(2,128)S(1)}, u32[]{:S(2)}, u32[]{:S(2)}) collective-permute-start(f32[3,20,2,128]{3,2,1,0:T(2,128)S(1)} %get-tuple-element.55), channel_id=1, source_target_pairs={{1,0},{2,1},{3,2},{4,3},{5,4},{6,5},{7,6},{8,7},{9,8},{10,9},{11,1... | collective-permute-start | bytes 184328 | tf_op jit(solution)/shard_map/ppermute | solution.py:24
  82.5 0.9 %copy-start = (f32[16,16,128]{2,1,0:T(8,128)S(1)}, f32[16,16,128]{2,1,0:T(8,128)}, u32[]{:S(2)}) copy-start(f32[16,16,128]{2,1,0:T(8,128)} %param.15) | copy-start | bytes 393220
  82.5 1.0 %copy-start.4 = (f32[16,16,128]{2,1,0:T(8,128)S(1)}, f32[16,16,128]{2,1,0:T(8,128)}, u32[]{:S(2)}) copy-start(f32[16,16,128]{2,1,0:T(8,128)} %param.14) | copy-start | bytes 393220
  84.5 0.9 %copy-start.6 = (f32[6,16,16,128]{3,2,1,0:T(8,128)}, f32[6,16,16,128]{3,2,1,0:T(8,128)S(1)}, u32[]{:S(2)}) copy-start(f32[6,16,16,128]{3,2,1,0:T(8,128)S(1)} %fusion.45) | copy-start | bytes 2359300
where the time goes:
time: 85.9 us; the launch traced here: 85.4 us
  starting transfers between devices  62.1 us (72%)
  other arithmetic  8.38 us (10%)
  local copies, waits for them, and re-layouts  6.26 us (7%)
  waiting for transfers between devices  5.42 us (6%)
  between operations  1.78 us (2%)
  matrix products  1.45 us (2%)
    ppermute x6, starting transfers between devices, with_halo(): lax.ppermute(head, axis, [((i + 1) % count, i) for i in range(ends)])  48.1 us
    ppermute x6, starting transfers between devices, with_halo(): lax.ppermute(tail, axis, [(i, (i + 1) % count) for i in range(ends)])  14 us
    ppermute x6, waiting for transfers between devices, with_halo(): lax.ppermute(head, axis, [((i + 1) % count, i) for i in range(ends)])  5.15 us
    slice x10, local copies, waits for them, and re-layouts, part(): return lax.slice_in_dim(padded, low, low + count, axis=axis)  2.48 us
    unnamed x19, local copies, waits for them, and re-layouts  2.2 us
    add x3, other arithmetic, factor(): total = total + table[k] * (offset == k).astype(jnp.float32)  2.06 us
    concatenate x2, other arithmetic, with_halo(): jnp.concatenate([lax.ppermute(tail, axis, [(i, (i + 1) % count) for i in...  2.05 us
  transfers between devices with their start and end apart: 12, of which 4 were waited for; matrix products, arithmetic and copies ran while one was open for 11% of the time, Pallas kernels for 0%

commit v1 on v0

v1 whole, which is shorter than its diff:
```python
import functools
import jax
import jax.numpy as jnp
from jax import lax
from jax.sharding import PartitionSpec as P
import jax.experimental.pallas as pl
import jax.experimental.pallas.tpu as pltpu

MESH = pl.DeviceIdType.MESH
F32 = jnp.float32
BF16 = jnp.bfloat16

c1 = 9.0 / 8.0
c2 = -1.0 / 24.0
time_step = 0.1
d_table = (1.0, -27.0, 27.0, -1.0)
w_table = (-1.0, 9.0, 9.0, -1.0)
unscale = 1.0 / (16.0 * 16.0 * 24.0)
pairs = ((0, 3, 4), (3, 1, 5), (4, 5, 2))
neighbours = ((-1, -1), (-1, 0), (-1, 1), (0, -1), (0, 1), (1, -1), (1, 0), (1, 1))


def lookup(offset, table):
    value = jnp.where(offset == 3, table[3], 0.0)
    for k in (2, 1, 0):
        value = jnp.where(offset == k, table[k], value)
    return value


def halves(low, high):
    lane = lax.broadcasted_iota(jnp.int32, (1, 128), 1)
    return jnp.where(lane < 64, low, high)


def stencil(length, start, position, table):
    cell = lax.broadcasted_iota(jnp.int32, (length, 128), 0) + start
    return lookup(cell - position + 1, table)


def depth_weights(pz):
    table = [halves(w, d) for w, d in zip(w_table, d_table)]
    weights = stencil(128, 0, pz, table).astype(BF16)
    return jnp.concatenate([weights, weights], axis=1)


def split(value):
    high = value.astype(BF16)
    low = (value - high.astype(F32)).astype(BF16)
    return jnp.concatenate([high, low], axis=1)


def cell_weights(slots, start_x, count_x, start_y, count_y, shift, y_major=False):
    px = slots[6:7, :].astype(jnp.int32) + shift[0]
    py = slots[7:8, :].astype(jnp.int32) + shift[1]
    mixed = [halves(d, w) for w, d in zip(w_table, d_table)]
    xa = stencil(count_x, start_x, px, mixed)
    xb = stencil(count_x, start_x, px, w_table)
    ya = stencil(count_y, start_y, py, w_table)
    yb = stencil(count_y, start_y, py, d_table)
    parts = []
    for i in range(3):
        p = slots[i : i + 1, :]
        q = slots[3 + i : 4 + i, :]
        if y_major:
            one, two = p * ya, q * yb
            rows = [one[k : k + 1, :] * xa + two[k : k + 1, :] * xb for k in range(count_y)]
        else:
            one, two = p * xa, q * xb
            rows = [one[k : k + 1, :] * ya + two[k : k + 1, :] * yb for k in range(count_x)]
        parts += rows
    return split(jnp.concatenate(parts, axis=0))


def matmul(left, right):
    return lax.dot_general(left, right, (((1,), (1,)), ((), ())), preferred_element_type=F32)


def diff(m2, m1, f, p1):
    return c1 * (f - m1) + c2 * (p1 - m2)


def along_y(f, low2, low1, high1, high2, forward):
    iy = lax.broadcasted_iota(jnp.int32, f.shape, 0)
    m1 = jnp.where(iy == 0, low1, pltpu.roll(f, 1, 0))
    p1 = jnp.where(iy == 15, high1, pltpu.roll(f, 15, 0))
    if forward:
        p2 = jnp.where(iy == 15, high2, jnp.where(iy == 14, high1, pltpu.roll(f, 14, 0)))
        return diff(m1, f, p1, p2)
    m2 = jnp.where(iy == 0, low2, jnp.where(iy == 1, low1, pltpu.roll(f, 2, 0)))
    return diff(m2, m1, f, p1)


def along_z(f, forward):
    iz = lax.broadcasted_iota(jnp.int32, f.shape, 1)
    m1 = jnp.where(iz < 1, 0.0, pltpu.roll(f, 1, 1))
    p1 = jnp.where(iz > 126, 0.0, pltpu.roll(f, 127, 1))
    if forward:
        p2 = jnp.where(iz > 125, 0.0, pltpu.roll(f, 126, 1))
        return diff(m1, f, p1, p2)
    m2 = jnp.where(iz < 2, 0.0, pltpu.roll(f, 2, 1))
    return diff(m2, m1, f, p1)


def kernel(
    nx, ny,
    v_in, s_in, b_in, l_in, m_in, mom_in, sig_in, px_in, py_in, pz_in, cnt_in,
    nv, ns,
    vel, st, buo, lam, mu, mom, sig, px, py, pz,
    slots, slots_from, ysend, ylow, yhigh, force, u, uysend, uylow, uyhigh,
    load_sem, send_sem, recv_sem,
):
    gx, gy = lax.axis_index("gx"), lax.axis_index("gy")

    def there(dx, dy):
        ok = True
        for at, step, count in ((gx, dx, nx), (gy, dy, ny)):
            if step:
                ok = ok & (at > 0) if step < 0 else ok & (at < count - 1)
        return ok

    barrier = pltpu.get_barrier_semaphore()
    expected = 0
    for dx, dy in neighbours:
        expected = expected + there(dx, dy).astype(jnp.int32)

        @pl.when(there(dx, dy))
        def _():
            pl.semaphore_signal(barrier, inc=1, device_id=(gx + dx, gy + dy), device_id_type=MESH)

    loads = {}
    for k, (name, src, dst) in enumerate((
        ("mom", mom_in, mom), ("sig", sig_in, sig), ("px", px_in, px), ("py", py_in, py),
        ("pz", pz_in, pz),
        ("st", s_in, st.at[:, 2:18]), ("vel", v_in, vel), ("buo", b_in, buo),
        ("lam", l_in, lam), ("mu", m_in, mu),
    )):
        loads[name] = pltpu.make_async_copy(src, dst, load_sem.at[k])
        loads[name].start()

    @pl.when(gx == 0)
    def _():
        st[:, 0:2] = jnp.zeros((6, 2, 16, 128), F32)
        u[:, 0:2] = jnp.zeros((3, 2, 16, 128), F32)

    @pl.when(gx == nx - 1)
    def _():
        st[:, 18:20] = jnp.zeros((6, 2, 16, 128), F32)
        u[:, 18:20] = jnp.zeros((3, 2, 16, 128), F32)

    @pl.when(gy == 0)
    def _():
        ylow[...] = jnp.zeros((5, 16, 128), F32)
        uylow[...] = jnp.zeros((4, 16, 128), F32)

    @pl.when(gy == ny - 1)
    def _():
        yhigh[...] = jnp.zeros((4, 16, 128), F32)
        uyhigh[...] = jnp.zeros((5, 16, 128), F32)

    for k, (dx, dy) in enumerate(neighbours):
        @pl.when(jnp.logical_not(there(dx, dy)))
        def _():
            slots_from[k] = jnp.zeros((16, 128), F32)

    for name in ("mom", "sig", "px", "py", "pz"):
        loads[name].wait()
    lane = lax.broadcasted_iota(jnp.int32, (1, 64), 1)
    live = (lane < cnt_in[0, 0, 0]).astype(F32)
    scaled = sig[0] * live * (-unscale)
    amp = [mom[0, r] * scaled for r in range(6)]
    nothing = jnp.zeros((1, 64), F32)
    rows = [jnp.concatenate([amp[pairs[i][0]], amp[pairs[i][2]]], axis=1) for i in range(3)]
    rows += [jnp.concatenate([amp[pairs[i][1]], nothing], axis=1) for i in range(3)]
    for ref in (px, py, pz):
        at = ref[0].astype(F32)
        rows.append(jnp.concatenate([at, at], axis=1))
    for r, row in enumerate(rows):
        slots[r : r + 1, :] = row
    slots[9:16, :] = jnp.zeros((7, 128), F32)

    def remote(k, src, dst, dx, dy):
        return pltpu.make_async_remote_copy(
            src_ref=src, dst_ref=dst, send_sem=send_sem.at[k], recv_sem=recv_sem.at[k],
            device_id=(gx + dx, gy + dy), device_id_type=MESH,
        )

    first = []
    for k, (dx, dy) in enumerate(neighbours):
        first.append((remote(k, slots, slots_from.at[7 - k], dx, dy), dx, dy))
    first_x = [
        (remote(8, s_in.at[0:1, 15:16], st.at[0:1, 1:2], 1, 0), 1, 0),
        (remote(9, s_in.at[3:5, 14:16], st.at[3:5, 0:2], 1, 0), 1, 0),
        (remote(10, s_in.at[0:1, 0:2], st.at[0:1, 18:20], -1, 0), -1, 0),
        (remote(11, s_in.at[3:5, 0:1], st.at[3:5, 18:19], -1, 0), -1, 0),
    ]
    first_y = [
        (remote(12, ysend.at[0:5], ylow, 0, 1), 0, 1),
        (remote(13, ysend.at[5:9], yhigh, 0, -1), 0, -1),
    ]
    second_x = [
        (remote(14, u.at[0:1, 16:18], u.at[0:1, 0:2], 1, 0), 1, 0),
        (remote(15, u.at[1:3, 17:18], u.at[1:3, 1:2], 1, 0), 1, 0),
        (remote(16, u.at[0:1, 2:3], u.at[0:1, 18:19], -1, 0), -1, 0),
        (remote(17, u.at[1:3, 2:4], u.at[1:3, 18:20], -1, 0), -1, 0),
    ]
    second_y = [
        (remote(18, uysend.at[0:4], uylow, 0, 1), 0, 1),
        (remote(19, uysend.at[4:9], uyhigh, 0, -1), 0, -1),
    ]

    def start(copies):
        for copy, dx, dy in copies:
            @pl.when(there(dx, dy))
            def _():
                copy.start()

    def arrive(copies):
        for copy, dx, dy in copies:
            @pl.when(there(-dx, -dy))
            def _():
                copy.wait_recv()

    def sent(copies):
        for copy, dx, dy in copies:
            @pl.when(there(dx, dy))
            def _():
                copy.wait_send()

    loads["st"].wait()
    for k, (f, y) in enumerate(((3, 14), (3, 15), (1, 15), (5, 14), (5, 15), (3, 0), (1, 0), (1, 1), (5, 0))):
        ysend[k] = st[f, 2:18, y, :]

    pl.semaphore_wait(barrier, expected)
    start(first_y)
    start(first)
    start(first_x)

    own = matmul(cell_weights(slots[...], 0, 16, 0, 16, (0, 0)), depth_weights(slots[8:9, :].astype(jnp.int32)))
    force[...] = own.reshape(3, 16, 16, 128)

    arrive(first)
    near = {n: slots_from[k] for k, n in enumerate(neighbours)}
    deep = {n: depth_weights(near[n][8:9, :].astype(jnp.int32)) for n in neighbours}
    for dx, start_x, count_x in ((-1, 0, 2), (1, 15, 1)):
        total = 0.0
        for dy in (-1, 0, 1):
            n = (dx, dy)
            total = total + matmul(cell_weights(near[n], start_x, count_x, 0, 16, (16 * dx, 16 * dy)), deep[n])
        force[:, start_x : start_x + count_x] += total.reshape(3, count_x, 16, 128)
    for dy, start_y, count_y in ((-1, 0, 2), (1, 15, 1)):
        n = (0, dy)
        got = matmul(cell_weights(near[n], 0, 16, start_y, count_y, (0, 16 * dy), True), deep[n])
        for i in range(3):
            for y in range(count_y):
                r = (i * count_y + y) * 16
                force[i, :, start_y + y, :] += got[r : r + 16, :]

    loads["vel"].wait()
    loads["buo"].wait()
    arrive(first_x)
    arrive(first_y)

    def velocity_plane(x, _):
        p = x + 2

        def low(k):
            return ylow[k, pl.ds(x, 1), :]

        def high(k):
            return yhigh[k, pl.ds(x, 1), :]

        sxy, syy, szz, sxz, syz = st[3, p], st[1, p], st[2, p], st[4, p], st[5, p]
        ax = diff(st[0, p - 1], st[0, p], st[0, p + 1], st[0, p + 2])
        ax += along_y(sxy, low(0), low(1), high(0), None, False) + along_z(sxz, False)
        ay = diff(st[3, p - 2], st[3, p - 1], sxy, st[3, p + 1])
        ay += along_y(syy, None, low(2), high(1), high(2), True) + along_z(syz, False)
        az = diff(st[4, p - 2], st[4, p - 1], sxz, st[4, p + 1])
        az += along_y(syz, low(3), low(4), high(3), None, False) + along_z(szz, True)
        scale = time_step * buo[x]
        nx = vel[0, x] + scale * (ax + force[0, x])
        u[0, p] = nx
        nv[0, x] = nx
        ny = vel[1, x] + scale * (ay + force[1, x])
        u[1, p] = ny
        nv[1, x] = ny
        nz = vel[2, x] + scale * (az + force[2, x])
        u[2, p] = nz
        nv[2, x] = nz
        return 0

    lax.fori_loop(0, 16, velocity_plane, 0)
    for k, (f, y) in enumerate(((0, 15), (1, 14), (1, 15), (2, 15), (0, 0), (0, 1), (1, 0), (2, 0), (2, 1))):
        uysend[k] = u[f, 2:18, y, :]
    start(second_y)
    start(second_x)

    loads["lam"].wait()
    loads["mu"].wait()
    arrive(second_x)
    arrive(second_y)

    def stress_plane(x, _):
        p = x + 2

        def low(k):
            return uylow[k, pl.ds(x, 1), :]

        def high(k):
            return uyhigh[k, pl.ds(x, 1), :]

        ux, uy, uz = u[0, p], u[1, p], u[2, p]
        exx = diff(u[0, p - 2], u[0, p - 1], ux, u[0, p + 1])
        eyy = along_y(uy, low(1), low(2), high(2), None, False)
        ezz = along_z(uz, False)
        two = (2.0 * time_step) * mu[x]
        press = time_step * lam[x] * (exx + eyy + ezz)
        shear = time_step * mu[x]
        ns[0, x] = st[0, p] + (press + two * exx)
        ns[1, x] = st[1, p] + (press + two * eyy)
        ns[2, x] = st[2, p] + (press + two * ezz)
        ns[3, x] = st[3, p] + shear * (
            along_y(ux, None, low(0), high(0), high(1), True)
            + diff(u[1, p - 1], uy, u[1, p + 1], u[1, p + 2])
        )
        ns[4, x] = st[4, p] + shear * (along_z(ux, True) + diff(u[2, p - 1], uz, u[2, p + 1], u[2, p + 2]))
        ns[5, x] = st[5, p] + shear * (along_z(uy, True) + along_y(uz, None, low(3), high(3), high(4), True))
        return 0

    lax.fori_loop(0, 16, stress_plane, 0)
    for copies in (first, first_x, first_y, second_x, second_y):
        sent(copies)


def store(v, s, v_out, s_out, sem):
    copies = [pltpu.make_async_copy(v, v_out, sem.at[0]), pltpu.make_async_copy(s, s_out, sem.at[1])]
    for copy in copies:
        copy.start()
    for copy in copies:
        copy.wait()


def local(velocity, stress, buoyancy, lame_lambda, shear_modulus, moment, signal, sx, sy, sz, count, *, nx, ny):
    hbm = pl.BlockSpec(memory_space=pltpu.HBM)
    on_chip = pl.BlockSpec(memory_space=pltpu.VMEM)
    vmem = pltpu.VMEM
    keep = functools.partial(pltpu.with_memory_space_constraint, memory_space=pltpu.VMEM)
    leave = functools.partial(pltpu.with_memory_space_constraint, memory_space=pltpu.HBM)
    args = (velocity, stress, buoyancy, lame_lambda, shear_modulus, jnp.transpose(moment, (0, 2, 1, 3)), signal, sx, sy, sz)
    done = pl.pallas_call(
        functools.partial(kernel, nx, ny),
        out_shape=(vmem(velocity.shape, F32), vmem(stress.shape, F32)),
        in_specs=[hbm] * 10 + [pl.BlockSpec(memory_space=pltpu.SMEM)],
        out_specs=(on_chip, on_chip),
        scratch_shapes=[
            vmem((3, 16, 16, 128), F32),
            vmem((6, 20, 16, 128), F32),
            vmem((16, 16, 128), F32),
            vmem((16, 16, 128), F32),
            vmem((16, 16, 128), F32),
            vmem((1, 6, 1, 64), F32),
            vmem((1, 1, 64), F32),
            vmem((1, 1, 64), jnp.int32),
            vmem((1, 1, 64), jnp.int32),
            vmem((1, 1, 64), jnp.int32),
            vmem((16, 128), F32),
            vmem((8, 16, 128), F32),
            vmem((9, 16, 128), F32),
            vmem((5, 16, 128), F32),
            vmem((4, 16, 128), F32),
            vmem((3, 16, 16, 128), F32),
            vmem((3, 20, 16, 128), F32),
            vmem((9, 16, 128), F32),
            vmem((4, 16, 128), F32),
            vmem((5, 16, 128), F32),
            pltpu.SemaphoreType.DMA((11,)),
            pltpu.SemaphoreType.DMA((20,)),
            pltpu.SemaphoreType.DMA((20,)),
        ],
        compiler_params=pltpu.CompilerParams(
            collective_id=0, has_side_effects=True, vmem_limit_bytes=48 * 1024 * 1024
        ),
        name="elastic_step",
    )(*map(leave, args), count)
    return pl.pallas_call(
        store,
        out_shape=(pltpu.HBM(velocity.shape, F32), pltpu.HBM(stress.shape, F32)),
        in_specs=[on_chip] * 2,
        out_specs=(hbm, hbm),
        scratch_shapes=[pltpu.SemaphoreType.DMA((2,))],
        name="store_fields",
    )(*map(keep, done))


def solution(mesh):
    field = P(None, "gx", "gy", None)
    cells = P("gx", "gy", None)
    in_specs = (field, field, cells, cells, cells, P("gx", "gy", None, None)) + (cells,) * 5
    step = functools.partial(local, nx=mesh.shape["gx"], ny=mesh.shape["gy"])
    return jax.shard_map(step, mesh=mesh, in_specs=in_specs, out_specs=(field, field), check_vma=False)
```

time: 85.9 us -> 36 us (0.42)
  starting transfers between devices: 62.1 us -> 0 us
  Pallas kernels: 0 us -> 34.1 us
  other arithmetic: 8.38 us -> 0 us
  local copies, waits for them, and re-layouts: 6.26 us -> 0 us
  waiting for transfers between devices: 5.42 us -> 0 us
  matrix products: 1.45 us -> 0 us
    ppermute x12 -> x0, starting transfers between devices: 62.1 us -> none  [the longest x6 48.1 us: with_halo(): lax.ppermute(head, axis, [((i + 1) % count, i) for i in range(ends)])]
    pallas_call x0 -> x2, Pallas kernels: none -> 34.1 us  [the longest x1 33.1 us: local(): pl.pallas_call(functools.partial(kernel, nx, ny), out_shape=(vmem(velocit...]
    ppermute x12 -> x0, waiting for transfers between devices: 5.42 us -> none  [the longest x6 5.15 us: with_halo(): lax.ppermute(head, axis, [((i + 1) % count, i) for i in range(ends)])]
    slice x15 -> x0, local copies, waits for them, and re-layouts: 3.67 us -> none  [the longest x10 2.48 us: part(): return lax.slice_in_dim(padded, low, low + count, axis=axis)]
    add x7 -> x0, other arithmetic: 2.87 us -> none  [the longest x3 2.06 us: factor(): total = total + table[k] * (offset == k).astype(jnp.float32)]
    unnamed x19 -> x0, local copies, waits for them, and re-layouts: 2.2 us -> none
    concatenate x2 -> x0, other arithmetic: 2.05 us -> none  [with_halo(): jnp.concatenate([lax.ppermute(tail, axis, [(i, (i + 1) % count) for i in...]
    dot_general x1 -> x0, matrix products: 1.45 us -> none  [spread_sources(): jnp.dot(left.reshape(-1, 3 * count), right, precision=lax.Precision.HIGHE...]
  transfers between devices with their start and end apart: 12 -> 0, of which waited for: 4 -> 0; matrix products, arithmetic and copies ran while one was open for 11% -> 0% of each run, Pallas kernels for 0% -> 0%
where the time goes in v1:
time: 36 us; the launch traced here: 35.4 us
  Pallas kernels  34.1 us (95%)
  between operations  1.29 us (4%)
    pallas_call x1, Pallas kernels, local(): pl.pallas_call(functools.partial(kernel, nx, ny), out_shape=(vmem(velocit...  33.1 us
    pallas_call x1, Pallas kernels, local(): pl.pallas_call(store, out_shape=(pltpu.HBM(velocity.shape, F32), pltpu.HB...  1.03 us

profile of v1, /device:TPU:6, one launch (start us, length us, event | category | flops | bytes accessed | tf_op | source)
XLA Modules:
  0.0 35.4 jit_solution(1348498992652018603)
XLA Ops:
  1.3 33.1 %elastic_step.1 = (f32[3,16,16,128]{3,2,1,0:T(8,128)S(1)}, f32[6,16,16,128]{3,2,1,0:T(8,128)S(1)}) custom-call(f32[3,16,16,128]{3,2,1,0:T(8,128)} %v_in.1, f32[6,16,16,128]{3,2,1,0:T(8,128)} %s_in.1, f32[16,16,128]{2,1,0:T(8,128)} %b_in.1, f32[16,16,128]{2,1,0:T(8,128)} %l_in.1, f32[16,16,128]{2,1,0:T(8,128)} %m_in.1, f32[1,6,1,64]{3,2,1,0:T(1,128)} %bitcast.1, ...), custom_call_target="tpu_custom_call" | custom-call | tf_op jit(solution)/shard_map/elastic_step/pallas_call | solution.py:349
  34.4 1.0 %store_fields.1 = (f32[3,16,16,128]{3,2,1,0:T(8,128)}, f32[6,16,16,128]{3,2,1,0:T(8,128)}) custom-call(f32[3,16,16,128]{3,2,1,0:T(8,128)S(1)} %get-tuple-element.4.v, f32[6,16,16,128]{3,2,1,0:T(8,128)S(1)} %get-tuple-element.5.s), custom_call_target="tpu_custom_call" | custom-call | tf_op jit(solution)/shard_map/store_fields/pallas_call | solution.py:384

commit v2 on v1

v2 whole, which is shorter than its diff:
```python
import functools
import jax
import jax.numpy as jnp
from jax import lax
from jax.sharding import PartitionSpec as P
import jax.experimental.pallas as pl
import jax.experimental.pallas.tpu as pltpu

MESH = pl.DeviceIdType.MESH
F32 = jnp.float32
BF16 = jnp.bfloat16

c1 = 9.0 / 8.0
c2 = -1.0 / 24.0
time_step = 0.1
d_table = (1.0, -27.0, 27.0, -1.0)
w_table = (-1.0, 9.0, 9.0, -1.0)
unscale = 1.0 / (16.0 * 16.0 * 24.0)
pairs = ((0, 3, 4), (3, 1, 5), (4, 5, 2))
neighbours = ((-1, -1), (-1, 0), (-1, 1), (0, -1), (0, 1), (1, -1), (1, 0), (1, 1))


stress_of_p = (("n", 15), ("t", 14), ("t", 15), ("r", 14), ("r", 15))
stress_of_q = (("n", 0), ("n", 1), ("t", 0), ("r", 0))
speed_of_p = (("n", 14), ("n", 15), ("t", 15), ("r", 15))
speed_of_q = (("n", 0), ("t", 0), ("t", 1), ("r", 0), ("r", 1))
component = ({"n": 0, "t": 1, "r": 2}, {"n": 1, "t": 0, "r": 2})
field = ({"n": 0, "t": 3, "r": 4}, {"n": 1, "t": 3, "r": 5})
role = tuple({c: r for r, c in names.items()} for names in component)
head = 8
order = ((0, 1), (1, 1), (-1, 1), (1, 0), (-1, 0), (1, -1), (-1, -1), (0, -1))


def give(get, upward):
    if upward:
        return {
            ("n", 0): lambda: -c2 * get("n", 15),
            ("t", 0): lambda: -c1 * get("t", 15) - c2 * get("t", 14),
            ("t", 1): lambda: -c2 * get("t", 15),
            ("r", 0): lambda: -c1 * get("r", 15) - c2 * get("r", 14),
            ("r", 1): lambda: -c2 * get("r", 15),
        }
    return {
        ("n", 14): lambda: c2 * get("n", 0),
        ("n", 15): lambda: c1 * get("n", 0) + c2 * get("n", 1),
        ("t", 15): lambda: c2 * get("t", 0),
        ("r", 15): lambda: c2 * get("r", 0),
    }


def corner_cells(sx, sy):
    cells = []
    for axis, (across, along) in enumerate(((sx, sy), (sy, sx))):
        other = 1 - axis
        for name, at in speed_of_p if across < 0 else speed_of_q:
            part = role[other][component[axis][name]]
            for what, index in stress_of_p if along < 0 else stress_of_q:
                if what == part:
                    cell = (field[other][what], at, index) if axis == 0 else (field[other][what], index, at)
                    if cell not in cells:
                        cells.append(cell)
    return cells


def lookup(offset, table):
    value = jnp.where(offset == 3, table[3], 0.0)
    for k in (2, 1, 0):
        value = jnp.where(offset == k, table[k], value)
    return value


def halves(low, high):
    lane = lax.broadcasted_iota(jnp.int32, (1, 128), 1)
    return jnp.where(lane < 64, low, high)


def stencil(length, start, position, table):
    cell = lax.broadcasted_iota(jnp.int32, (length, 128), 0) + start
    return lookup(cell - position + 1, table)


def unpack(rows):
    p = [rows[i : i + 1, :] for i in range(3)]
    mixed = [rows[3 + i : 4 + i, :] for i in range(3)]
    q = [halves(row, 0.0) for row in mixed]
    at = [halves(pltpu.roll(row, 64, 1), row).astype(jnp.int32) for row in mixed]
    return p, q, at


def depth_weights(pz):
    table = [halves(w, d) for w, d in zip(w_table, d_table)]
    weights = stencil(128, 0, pz, table).astype(BF16)
    return jnp.concatenate([weights, weights], axis=1)


def spread(tile, shift, pieces):
    p, q, (px, py, pz) = tile
    mixed = [halves(d, w) for w, d in zip(w_table, d_table)]
    position = (px + 16 * shift[0], py + 16 * shift[1])
    tables = ((mixed, w_table), (w_table, d_table))
    rows = []
    for axis, layers, start, count in pieces:
        one = [stencil(len(layers), layers[0], position[axis], table) for table in tables[axis]]
        two = [stencil(count, start, position[1 - axis], table) for table in tables[1 - axis]]
        for i in range(3):
            first, second = p[i] * one[0], q[i] * one[1]
            for k in range(len(layers)):
                rows.append(first[k : k + 1, :] * two[0] + second[k : k + 1, :] * two[1])
    value = jnp.concatenate(rows, axis=0)
    high = value.astype(BF16)
    low = (value - high.astype(F32)).astype(BF16)
    result = lax.dot_general(
        jnp.concatenate([high, low], axis=1), depth_weights(pz), (((1,), (1,)), ((), ())),
        preferred_element_type=F32,
    )
    parts, at = [], 0
    for axis, layers, start, count in pieces:
        size = 3 * len(layers) * count
        parts.append(result[at : at + size])
        at += size
    return parts


def diff(m2, m1, f, p1):
    return c1 * (f - m1) + c2 * (p1 - m2)


def along_y(f, low2, low1, high1, high2, forward):
    iy = lax.broadcasted_iota(jnp.int32, f.shape, 0)
    m1 = jnp.where(iy == 0, low1, pltpu.roll(f, 1, 0))
    p1 = jnp.where(iy == 15, high1, pltpu.roll(f, 15, 0))
    if forward:
        p2 = jnp.where(iy == 15, high2, jnp.where(iy == 14, high1, pltpu.roll(f, 14, 0)))
        return diff(m1, f, p1, p2)
    m2 = jnp.where(iy == 0, low2, jnp.where(iy == 1, low1, pltpu.roll(f, 2, 0)))
    return diff(m2, m1, f, p1)


def along_z(f, forward):
    iz = lax.broadcasted_iota(jnp.int32, f.shape, 1)
    m1 = jnp.where(iz < 1, 0.0, pltpu.roll(f, 1, 1))
    p1 = jnp.where(iz > 126, 0.0, pltpu.roll(f, 127, 1))
    if forward:
        p2 = jnp.where(iz > 125, 0.0, pltpu.roll(f, 126, 1))
        return diff(m1, f, p1, p2)
    m2 = jnp.where(iz < 2, 0.0, pltpu.roll(f, 2, 1))
    return diff(m2, m1, f, p1)


def planes(plane):
    def group(i, _):
        for k in range(4):
            plane(i * 4 + k)
        return 0

    lax.fori_loop(0, 4, group, 0)


def kernel(
    nx, ny,
    v_in, s_in, b_in, l_in, m_in, mom_in, sig_in, px_in, py_in, pz_in, cnt_in,
    nv, ns,
    vel, st, buo, lam, mu, mom, sig, px, py, pz,
    force, u, forces, face_out, face_in, speed_out, speed_in, corner_out, corner_in,
    load_sem, send_sem, recv_sem,
):
    gx, gy = lax.axis_index("gx"), lax.axis_index("gy")

    def there(dx, dy):
        ok = True
        for at, step, count in ((gx, dx, nx), (gy, dy, ny)):
            if step:
                ok = ok & (at > 0) if step < 0 else ok & (at < count - 1)
        return ok

    barrier = pltpu.get_barrier_semaphore()
    expected = 0
    for dx, dy in neighbours:
        expected = expected + there(dx, dy).astype(jnp.int32)

        @pl.when(there(dx, dy))
        def _():
            pl.semaphore_signal(barrier, inc=1, device_id=(gx + dx, gy + dy), device_id_type=MESH)

    loads = {}
    for k, (name, src, dst) in enumerate((
        ("mom", mom_in, mom), ("sig", sig_in, sig), ("px", px_in, px), ("py", py_in, py),
        ("pz", pz_in, pz),
        ("st", s_in, st.at[:, 2:18]), ("vel", v_in, vel), ("buo", b_in, buo),
        ("lam", l_in, lam), ("mu", m_in, mu),
    )):
        loads[name] = pltpu.make_async_copy(src, dst, load_sem.at[k])
        loads[name].start()

    sides = ((-1, 0), (1, 0), (0, -1), (0, 1))
    corners = ((-1, -1), (-1, 1), (1, -1), (1, 1))
    lists = {n: corner_cells(*n) for n in corners}

    for f in (0, 3, 4):
        st[f, 0:2] = jnp.zeros((2, 16, 128), F32)
        st[f, 18:20] = jnp.zeros((2, 16, 128), F32)
    forces[...] = jnp.zeros((8, 3, 2, 16, 128), F32)
    for k, n in enumerate(sides):
        @pl.when(jnp.logical_not(there(*n)))
        def _():
            face_in[k] = jnp.zeros((120, 128), F32)
            speed_in[k] = jnp.zeros((5, 16, 128), F32)

    for k, n in enumerate(corners):
        @pl.when(jnp.logical_not(there(*n)))
        def _():
            corner_in[k] = jnp.zeros((24, 128), F32)

    for name in ("mom", "sig", "px", "py", "pz"):
        loads[name].wait()
    lane = lax.broadcasted_iota(jnp.int32, (1, 64), 1)
    live = (lane < cnt_in[0, 0, 0]).astype(F32)
    scaled = sig[0] * live * (-unscale)
    amp = [mom[0, r] * scaled for r in range(6)]
    rows = [jnp.concatenate([amp[pairs[i][0]], amp[pairs[i][2]]], axis=1) for i in range(3)]
    for i, ref in enumerate((px, py, pz)):
        rows.append(jnp.concatenate([amp[pairs[i][1]], ref[0].astype(F32)], axis=1))
    own_rows = jnp.concatenate(rows, axis=0)
    for k in range(4):
        face_out[k, 0:6, :] = own_rows
        face_out[k, 6:8, :] = jnp.zeros((2, 128), F32)
        corner_out[k, 0:6, :] = own_rows

    def remote(k, src, dst, n):
        return pltpu.make_async_remote_copy(
            src_ref=src, dst_ref=dst, send_sem=send_sem.at[k], recv_sem=recv_sem.at[k],
            device_id=(gx + n[0], gy + n[1]), device_id_type=MESH,
        )

    copies = {}
    for k, n in enumerate(sides):
        upward = k % 2 == 1
        size = head + 16 * (len(stress_of_p if upward else stress_of_q) + 2)
        count = len(speed_of_p if upward else speed_of_q)
        back = (-n[0], -n[1])
        copies["face", back] = remote(k, face_out.at[k, 0:size], face_in.at[k ^ 1, 0:size], n)
        copies["speed", back] = remote(4 + k, speed_out.at[k, 0:count], speed_in.at[k ^ 1, 0:count], n)
    for k, n in enumerate(corners):
        back = (-n[0], -n[1])
        size = -(-(6 + len(lists[back])) // 8) * 8
        copies["corner", back] = remote(8 + k, corner_out.at[k, 0:size], corner_in.at[3 - k, 0:size], n)

    def start(kind):
        for (what, back), copy in copies.items():
            if what == kind:
                @pl.when(there(-back[0], -back[1]))
                def _():
                    copy.start()

    def arrive(kind, n):
        @pl.when(there(*n))
        def _():
            copies[kind, n].wait_recv()

    def layer(ref, axis, f, at):
        return ref[f, at + 2] if axis == 0 else ref[f, 2:18, at, :]

    loads["st"].wait()
    loads["buo"].wait()
    for k in range(4):
        axis, upward = k // 2, k % 2 == 1
        at = head
        for name, index in stress_of_p if upward else stress_of_q:
            face_out[k, at : at + 16, :] = layer(st, axis, field[axis][name], index)
            at += 16
        for index in (14, 15) if upward else (0, 1):
            face_out[k, at : at + 16, :] = buo[index] if axis == 0 else buo[:, index, :]
            at += 16
    for k, n in enumerate(corners):
        for r, (f, x, y) in enumerate(lists[-n[0], -n[1]]):
            corner_out[k, 6 + r : 7 + r, :] = st[f, 2 + x, y : y + 1, :]
        if 6 + len(lists[-n[0], -n[1]]) > 16:
            corner_out[k, 6 + len(lists[-n[0], -n[1]]) : 24, :] = jnp.zeros((18 - len(lists[-n[0], -n[1]]), 128), F32)

    pl.semaphore_wait(barrier, expected)
    start("face")
    start("corner")

    me = unpack(own_rows)
    force[...] = spread(me, (0, 0), [(0, tuple(range(16)), 0, 16)])[0].reshape(3, 16, 16, 128)
    loads["vel"].wait()

    def velocity_plane(x):
        p = x + 2
        sxy, syy, szz, sxz, syz = st[3, p], st[1, p], st[2, p], st[4, p], st[5, p]
        ax = diff(st[0, p - 1], st[0, p], st[0, p + 1], st[0, p + 2])
        ax += along_y(sxy, 0.0, 0.0, 0.0, 0.0, False) + along_z(sxz, False)
        ay = diff(st[3, p - 2], st[3, p - 1], sxy, st[3, p + 1])
        ay += along_y(syy, 0.0, 0.0, 0.0, 0.0, True) + along_z(syz, False)
        az = diff(st[4, p - 2], st[4, p - 1], sxz, st[4, p + 1])
        az += along_y(syz, 0.0, 0.0, 0.0, 0.0, False) + along_z(szz, True)
        scale = time_step * buo[x]
        u[0, p] = vel[0, x] + scale * (ax + force[0, x])
        u[1, p] = vel[1, x] + scale * (ay + force[1, x])
        u[2, p] = vel[2, x] + scale * (az + force[2, x])

    planes(velocity_plane)
    for k in range(4):
        axis, upward = k // 2, k % 2 == 1
        for at, (name, index) in enumerate(speed_of_p if upward else speed_of_q):
            speed_out[k, at] = layer(u, axis, component[axis][name], index)
    start("speed")

    def add_force(tile, n, pieces):
        parts = spread(tile, n, [piece for _, piece in pieces])
        for (region, (axis, layers, first, count)), part in zip(pieces, parts):
            base = {0: 0, 1: 14, 2: -2, 3: 16}[region % 2 + 2 * (region // 4)]
            at = 0
            for i in range(3):
                for a in layers:
                    forces[region, i, a - base, first : first + count, :] += part[at : at + count]
                    at += count

    every = (0, 16)
    block = {-1: (0, 8), 0: every, 1: (8, 8)}
    add_force(me, (0, 0), [
        (4, (0, (-1,), *every)), (5, (0, (16, 17), *every)), (6, (1, (-1,), *every)), (7, (1, (16, 17), *every)),
    ])
    low_in, high_in, low_out, high_out = (0, 1), (15,), (-2, -1), (16, 17)
    for n in order:
        tx, ty = n
        if tx and ty:
            arrive("corner", n)
            tile = unpack(corner_in[corners.index(n), 0:8, :])
        else:
            arrive("face", n)
            tile = unpack(face_in[sides.index(n), 0:8, :])
        pieces = []
        if tx:
            pieces.append((0 if tx < 0 else 1, (0, low_in if tx < 0 else high_in, *block[ty])))
            for sy in ((-1, 1) if ty == 0 else (ty,)):
                layers = (low_out if sy < 0 else high_out) if ty else ((-1,) if sy < 0 else (16, 17))
                pieces.append((6 if sy < 0 else 7, (1, layers, *block[tx])))
        else:
            pieces.append((2 if ty < 0 else 3, (1, low_in if ty < 0 else high_in, *every)))
        if ty:
            for sx in ((-1, 1) if tx == 0 else (tx,)):
                layers = (low_out if sx < 0 else high_out) if tx else ((-1,) if sx < 0 else (16, 17))
                pieces.append((4 if sx < 0 else 5, (0, layers, *block[ty])))
        add_force(tile, n, pieces)

    row = lax.broadcasted_iota(jnp.int32, (16, 128), 0)
    for k in (3, 1, 0, 2):
        axis, upward = k // 2, k % 2 == 1
        names = component[axis]
        mine = lambda name, index: layer(st, axis, field[axis][name], index)
        layers = stress_of_q if upward else stress_of_p
        theirs = lambda name, index: face_in[k, pl.ds(head + 16 * layers.index((name, index)), 16), :]
        added = give(theirs, not upward)
        base = 14 if upward else 0
        for name in ("n", "t", "r"):
            c = names[name]
            for index in (base, base + 1):
                if upward and index == 14 and name != "n":
                    continue
                acc = forces[k, c, index - base]
                if (name, index) in added:
                    acc = acc + added[name, index]()
                if axis == 0:
                    u[c, 2 + index] += time_step * buo[index] * acc
                else:
                    u[c, 2:18, index, :] = u[c, 2:18, index, :] + time_step * buo[:, index, :] * acc
        arrive("speed", sides[k])
        added = give(mine, upward)
        other = 1 - axis
        for at, (name, index) in enumerate(speed_of_q if upward else speed_of_p):
            c = names[name]
            near = index if upward else index - 14
            acc = forces[4 + k, c, near] + added[name, index]()
            for along in (-1, 1):
                n = (sides[k][0] + (0 if axis == 0 else along), sides[k][1] + (along if axis == 0 else 0))
                cells = lists[n]

                def cell(what, where):
                    key = (field[other][what], index, where) if axis == 0 else (field[other][what], where, index)
                    r = 6 + cells.index(key)
                    return corner_in[corners.index(n), r : r + 1, :]

                for (what, where), value in give(cell, along < 0).items():
                    if what == role[other][c]:
                        acc = acc + jnp.where(row == where, value(), 0.0)
            b_at = head + 16 * (len(layers) + near)
            total = speed_in[k, at] + time_step * face_in[k, b_at : b_at + 16, :] * acc
            if axis == 0:
                u[c, (18 if upward else 0) + near] = total
            else:
                speed_in[k, at] = total

    loads["lam"].wait()
    loads["mu"].wait()

    def stress_plane(x):
        p = x + 2

        def low(k):
            return speed_in[2, k, pl.ds(x, 1), :]

        def high(k):
            return speed_in[3, k, pl.ds(x, 1), :]

        ux, uy, uz = u[0, p], u[1, p], u[2, p]
        nv[0, x], nv[1, x], nv[2, x] = ux, uy, uz
        exx = diff(u[0, p - 2], u[0, p - 1], ux, u[0, p + 1])
        eyy = along_y(uy, low(0), low(1), high(0), None, False)
        ezz = along_z(uz, False)
        two = (2.0 * time_step) * mu[x]
        press = time_step * lam[x] * (exx + eyy + ezz)
        shear = time_step * mu[x]
        ns[0, x] = st[0, p] + (press + two * exx)
        ns[1, x] = st[1, p] + (press + two * eyy)
        ns[2, x] = st[2, p] + (press + two * ezz)
        ns[3, x] = st[3, p] + shear * (
            along_y(ux, None, low(2), high(1), high(2), True)
            + diff(u[1, p - 1], uy, u[1, p + 1], u[1, p + 2])
        )
        ns[4, x] = st[4, p] + shear * (along_z(ux, True) + diff(u[2, p - 1], uz, u[2, p + 1], u[2, p + 2]))
        ns[5, x] = st[5, p] + shear * (along_z(uy, True) + along_y(uz, None, low(3), high(3), high(4), True))

    planes(stress_plane)
    for (what, back), copy in copies.items():
        @pl.when(there(-back[0], -back[1]))
        def _():
            copy.wait_send()


def store(v, s, v_out, s_out, sem):
    copies = [pltpu.make_async_copy(v, v_out, sem.at[0]), pltpu.make_async_copy(s, s_out, sem.at[1])]
    for copy in copies:
        copy.start()
    for copy in copies:
        copy.wait()


def local(velocity, stress, buoyancy, lame_lambda, shear_modulus, moment, signal, sx, sy, sz, count, *, nx, ny):
    hbm = pl.BlockSpec(memory_space=pltpu.HBM)
    on_chip = pl.BlockSpec(memory_space=pltpu.VMEM)
    vmem = pltpu.VMEM
    keep = functools.partial(pltpu.with_memory_space_constraint, memory_space=pltpu.VMEM)
    leave = functools.partial(pltpu.with_memory_space_constraint, memory_space=pltpu.HBM)
    args = (velocity, stress, buoyancy, lame_lambda, shear_modulus, jnp.transpose(moment, (0, 2, 1, 3)), signal, sx, sy, sz)
    done = pl.pallas_call(
        functools.partial(kernel, nx, ny),
        out_shape=(vmem(velocity.shape, F32), vmem(stress.shape, F32)),
        in_specs=[hbm] * 10 + [pl.BlockSpec(memory_space=pltpu.SMEM)],
        out_specs=(on_chip, on_chip),
        scratch_shapes=[
            vmem((3, 16, 16, 128), F32),
            vmem((6, 20, 16, 128), F32),
            vmem((16, 16, 128), F32),
            vmem((16, 16, 128), F32),
            vmem((16, 16, 128), F32),
            vmem((1, 6, 1, 64), F32),
            vmem((1, 1, 64), F32),
            vmem((1, 1, 64), jnp.int32),
            vmem((1, 1, 64), jnp.int32),
            vmem((1, 1, 64), jnp.int32),
            vmem((3, 16, 16, 128), F32),
            vmem((3, 20, 16, 128), F32),
            vmem((8, 3, 2, 16, 128), F32),
            vmem((4, 120, 128), F32),
            vmem((4, 120, 128), F32),
            vmem((4, 5, 16, 128), F32),
            vmem((4, 5, 16, 128), F32),
            vmem((4, 24, 128), F32),
            vmem((4, 24, 128), F32),
            pltpu.SemaphoreType.DMA((10,)),
            pltpu.SemaphoreType.DMA((12,)),
            pltpu.SemaphoreType.DMA((12,)),
        ],
        compiler_params=pltpu.CompilerParams(
            collective_id=0, has_side_effects=True, vmem_limit_bytes=48 * 1024 * 1024
        ),
        name="elastic_step",
    )(*map(leave, args), count)
    return pl.pallas_call(
        store,
        out_shape=(pltpu.HBM(velocity.shape, F32), pltpu.HBM(stress.shape, F32)),
        in_specs=[on_chip] * 2,
        out_specs=(hbm, hbm),
        scratch_shapes=[pltpu.SemaphoreType.DMA((2,))],
        name="store_fields",
    )(*map(keep, done))


def solution(mesh):
    field = P(None, "gx", "gy", None)
    cells = P("gx", "gy", None)
    in_specs = (field, field, cells, cells, cells, P("gx", "gy", None, None)) + (cells,) * 5
    step = functools.partial(local, nx=mesh.shape["gx"], ny=mesh.shape["gy"])
    return jax.shard_map(step, mesh=mesh, in_specs=in_specs, out_specs=(field, field), check_vma=False)
```

time: 36 us -> 29 us (0.81)
  the two profiles are of different devices: /device:TPU:6 before, /device:TPU:31 now
where the time goes in v2:
time: 29 us; the launch traced here: 28.8 us
  Pallas kernels  27.5 us (95%)
  between operations  1.29 us (4%)
    pallas_call x1, Pallas kernels, local(): pl.pallas_call(functools.partial(kernel, nx, ny), out_shape=(vmem(velocit...  26.5 us
    pallas_call x1, Pallas kernels, local(): pl.pallas_call(store, out_shape=(pltpu.HBM(velocity.shape, F32), pltpu.HB...  1.03 us

profile of v2, /device:TPU:31, one launch (start us, length us, event | category | flops | bytes accessed | tf_op | source)
XLA Modules:
  0.0 28.8 jit_solution(4672135711138346593)
XLA Ops:
  1.3 26.5 %elastic_step.1 = (f32[3,16,16,128]{3,2,1,0:T(8,128)S(1)}, f32[6,16,16,128]{3,2,1,0:T(8,128)S(1)}) custom-call(f32[3,16,16,128]{3,2,1,0:T(8,128)} %v_in.1, f32[6,16,16,128]{3,2,1,0:T(8,128)} %s_in.1, f32[16,16,128]{2,1,0:T(8,128)} %b_in.1, f32[16,16,128]{2,1,0:T(8,128)} %l_in.1, f32[16,16,128]{2,1,0:T(8,128)} %m_in.1, f32[1,6,1,64]{3,2,1,0:T(1,128)} %bitcast.1, ...), custom_call_target="tpu_custom_call" | custom-call | tf_op jit(solution)/shard_map/elastic_step/pallas_call | solution.py:446
  27.8 1.0 %store_fields.1 = (f32[3,16,16,128]{3,2,1,0:T(8,128)}, f32[6,16,16,128]{3,2,1,0:T(8,128)}) custom-call(f32[3,16,16,128]{3,2,1,0:T(8,128)S(1)} %get-tuple-element.4.v, f32[6,16,16,128]{3,2,1,0:T(8,128)S(1)} %get-tuple-element.5.s), custom_call_target="tpu_custom_call" | custom-call | tf_op jit(solution)/shard_map/store_fields/pallas_call | solution.py:480

commit v3 on v2

--- a/solution.py
+++ b/solution.py
@@ -28,7 +28,8 @@
 field = ({"n": 0, "t": 3, "r": 4}, {"n": 1, "t": 3, "r": 5})
 role = tuple({c: r for r, c in names.items()} for names in component)
 head = 8
-order = ((0, 1), (1, 1), (-1, 1), (1, 0), (-1, 0), (1, -1), (-1, -1), (0, -1))
+early = ((0, 1), (1, 1), (-1, 1), (1, 0), (-1, 0))
+late = ((1, -1), (-1, -1), (0, -1))
 
 
 def give(get, upward):
@@ -159,9 +160,9 @@
 def kernel(
     nx, ny,
     v_in, s_in, b_in, l_in, m_in, mom_in, sig_in, px_in, py_in, pz_in, cnt_in,
-    nv, ns,
-    vel, st, buo, lam, mu, mom, sig, px, py, pz,
-    force, u, forces, face_out, face_in, speed_out, speed_in, corner_out, corner_in,
+    u, st, lam, mu, edge,
+    vel, buo, mom, sig, px, py, pz,
+    force, forces, face_out, face_in, speed_out, speed_in, corner_out, corner_in,
     load_sem, send_sem, recv_sem,
 ):
     gx, gy = lax.axis_index("gx"), lax.axis_index("gy")
@@ -186,7 +187,7 @@
     for k, (name, src, dst) in enumerate((
         ("mom", mom_in, mom), ("sig", sig_in, sig), ("px", px_in, px), ("py", py_in, py),
         ("pz", pz_in, pz),
-        ("st", s_in, st.at[:, 2:18]), ("vel", v_in, vel), ("buo", b_in, buo),
+        ("st", s_in, st.at[:, 2:18]), ("buo", b_in, buo), ("vel", v_in, vel),
         ("lam", l_in, lam), ("mu", m_in, mu),
     )):
         loads[name] = pltpu.make_async_copy(src, dst, load_sem.at[k])
@@ -199,7 +200,7 @@
     for f in (0, 3, 4):
         st[f, 0:2] = jnp.zeros((2, 16, 128), F32)
         st[f, 18:20] = jnp.zeros((2, 16, 128), F32)
-    forces[...] = jnp.zeros((8, 3, 2, 16, 128), F32)
+    forces[...] = jnp.zeros((12, 3, 2, 16, 128), F32)
     for k, n in enumerate(sides):
         @pl.when(jnp.logical_not(there(*n)))
         def _():
@@ -306,10 +307,11 @@
             speed_out[k, at] = layer(u, axis, component[axis][name], index)
     start("speed")
 
-    def add_force(tile, n, pieces):
+    def add_force(tile, n, pieces, shelf=None):
         parts = spread(tile, n, [piece for _, piece in pieces])
         for (region, (axis, layers, first, count)), part in zip(pieces, parts):
             base = {0: 0, 1: 14, 2: -2, 3: 16}[region % 2 + 2 * (region // 4)]
+            region = (shelf or {}).get(region, region)
             at = 0
             for i in range(3):
                 for a in layers:
@@ -322,13 +324,13 @@
         (4, (0, (-1,), *every)), (5, (0, (16, 17), *every)), (6, (1, (-1,), *every)), (7, (1, (16, 17), *every)),
     ])
     low_in, high_in, low_out, high_out = (0, 1), (15,), (-2, -1), (16, 17)
-    for n in order:
+    shelf = {0: 8, 1: 9, 4: 10, 5: 11}
+
+    def tile_force(n):
         tx, ty = n
         if tx and ty:
-            arrive("corner", n)
             tile = unpack(corner_in[corners.index(n), 0:8, :])
         else:
-            arrive("face", n)
             tile = unpack(face_in[sides.index(n), 0:8, :])
         pieces = []
         if tx:
@@ -342,15 +344,44 @@
             for sx in ((-1, 1) if tx == 0 else (tx,)):
                 layers = (low_out if sx < 0 else high_out) if tx else ((-1,) if sx < 0 else (16, 17))
                 pieces.append((4 if sx < 0 else 5, (0, layers, *block[ty])))
-        add_force(tile, n, pieces)
+        add_force(tile, n, pieces, shelf if n in late else None)
+
+    def come(tiles):
+        for n in tiles:
+            arrive("corner" if n[0] and n[1] else "face", n)
+        for n in tiles:
+            tile_force(n)
+
+    def corner_share(k, name, index, along):
+        axis = k // 2
+        other = 1 - axis
+        n = (sides[k][0] + (0 if axis == 0 else along), sides[k][1] + (along if axis == 0 else 0))
+
+        def cell(what, where):
+            key = (field[other][what], index, where) if axis == 0 else (field[other][what], where, index)
+            r = 6 + lists[n].index(key)
+            return corner_in[corners.index(n), r : r + 1, :]
+
+        return [
+            (where, value())
+            for (what, where), value in give(cell, along < 0).items()
+            if what == role[other][component[axis][name]]
+        ]
 
     row = lax.broadcasted_iota(jnp.int32, (16, 128), 0)
-    for k in (3, 1, 0, 2):
+
+    def share(k):
         axis, upward = k // 2, k % 2 == 1
         names = component[axis]
-        mine = lambda name, index: layer(st, axis, field[axis][name], index)
         layers = stress_of_q if upward else stress_of_p
-        theirs = lambda name, index: face_in[k, pl.ds(head + 16 * layers.index((name, index)), 16), :]
+
+        def mine(name, index):
+            return layer(st, axis, field[axis][name], index)
+
+        def theirs(name, index):
+            at = head + 16 * layers.index((name, index))
+            return face_in[k, at : at + 16, :]
+
         added = give(theirs, not upward)
         base = 14 if upward else 0
         for name in ("n", "t", "r"):
@@ -367,44 +398,66 @@
                     u[c, 2:18, index, :] = u[c, 2:18, index, :] + time_step * buo[:, index, :] * acc
         arrive("speed", sides[k])
         added = give(mine, upward)
-        other = 1 - axis
         for at, (name, index) in enumerate(speed_of_q if upward else speed_of_p):
             c = names[name]
             near = index if upward else index - 14
             acc = forces[4 + k, c, near] + added[name, index]()
-            for along in (-1, 1):
-                n = (sides[k][0] + (0 if axis == 0 else along), sides[k][1] + (along if axis == 0 else 0))
-                cells = lists[n]
-
-                def cell(what, where):
-                    key = (field[other][what], index, where) if axis == 0 else (field[other][what], where, index)
-                    r = 6 + cells.index(key)
-                    return corner_in[corners.index(n), r : r + 1, :]
-
-                for (what, where), value in give(cell, along < 0).items():
-                    if what == role[other][c]:
-                        acc = acc + jnp.where(row == where, value(), 0.0)
+            for along in (1,) if axis == 0 else (-1, 1):
+                for where, value in corner_share(k, name, index, along):
+                    acc = acc + jnp.where(row == where, value, 0.0)
             b_at = head + 16 * (len(layers) + near)
             total = speed_in[k, at] + time_step * face_in[k, b_at : b_at + 16, :] * acc
             if axis == 0:
                 u[c, (18 if upward else 0) + near] = total
             else:
-                speed_in[k, at] = total
+                edge[k - 2, at] = total
+
+    def late_share(k):
+        upward = k == 1
+        for index in (15,) if upward else (0, 1):
+            for c in range(3):
+                acc = forces[shelf[k], c, index - (14 if upward else 0), 0:8, :]
+                u[c, 2 + index, 0:8, :] += time_step * buo[index, 0:8, :] * acc
+        for name, index in speed_of_q if upward else speed_of_p:
+            c = component[0][name]
+            near = index if upward else index - 14
+            acc = forces[shelf[4 + k], c, near, 0:8, :]
+            for where, value in corner_share(k, name, index, -1):
+                acc = acc + jnp.where(row[0:8] == where, value, 0.0)
+            b_at = head + 16 * (len(stress_of_q if upward else stress_of_p) + near)
+            u[c, (18 if upward else 0) + near, 0:8, :] += time_step * face_in[k, b_at : b_at + 8, :] * acc
+
+    come(early)
+    for k in (3, 1, 0):
+        share(k)
+    come(late)
+    for k in (1, 0):
+        late_share(k)
+    share(2)
 
     loads["lam"].wait()
     loads["mu"].wait()
 
+    for (what, back), copy in copies.items():
+        @pl.when(there(-back[0], -back[1]))
+        def _():
+            copy.wait_send()
+
+
+def finish(u, st, lam, mu, edge, v_out, s_out, ns, sem):
+    copies = [pltpu.make_async_copy(u.at[:, 2:18], v_out, sem.at[4])]
+    copies[0].start()
+
     def stress_plane(x):
         p = x + 2
 
         def low(k):
-            return speed_in[2, k, pl.ds(x, 1), :]
+            return edge[0, k, x : x + 1, :]
 
         def high(k):
-            return speed_in[3, k, pl.ds(x, 1), :]
+            return edge[1, k, x : x + 1, :]
 
         ux, uy, uz = u[0, p], u[1, p], u[2, p]
-        nv[0, x], nv[1, x], nv[2, x] = ux, uy, uz
         exx = diff(u[0, p - 2], u[0, p - 1], ux, u[0, p + 1])
         eyy = along_y(uy, low(0), low(1), high(0), None, False)
         ezz = along_z(uz, False)
@@ -421,19 +474,22 @@
         ns[4, x] = st[4, p] + shear * (along_z(ux, True) + diff(u[2, p - 1], uz, u[2, p + 1], u[2, p + 2]))
         ns[5, x] = st[5, p] + shear * (along_z(uy, True) + along_y(uz, None, low(3), high(3), high(4), True))
 
-    planes(stress_plane)
-    for (what, back), copy in copies.items():
-        @pl.when(there(-back[0], -back[1]))
-        def _():
-            copy.wait_send()
-
-
-def store(v, s, v_out, s_out, sem):
-    copies = [pltpu.make_async_copy(v, v_out, sem.at[0]), pltpu.make_async_copy(s, s_out, sem.at[1])]
-    for copy in copies:
-        copy.start()
+    for part in range(4):
+        cells = pl.ds(4 * part, 4)
+        for x in range(4 * part, 4 * part + 4):
+            stress_plane(x)
+        copies.append(pltpu.make_async_copy(ns.at[:, cells], s_out.at[:, cells], sem.at[part]))
+        copies[-1].start()
     for copy in copies:
         copy.wait()
+
+
+def kept(*shape):
+    return pltpu.VMEM(shape, F32)
+
+
+def result(shape):
+    return pltpu.HBM(shape, F32)
 
 
 def local(velocity, stress, buoyancy, lame_lambda, shear_modulus, moment, signal, sx, sy, sz, count, *, nx, ny):
@@ -445,14 +501,11 @@
     args = (velocity, stress, buoyancy, lame_lambda, shear_modulus, jnp.transpose(moment, (0, 2, 1, 3)), signal, sx, sy, sz)
     done = pl.pallas_call(
         functools.partial(kernel, nx, ny),
-        out_shape=(vmem(velocity.shape, F32), vmem(stress.shape, F32)),
+        out_shape=(kept(3, 20, 16, 128), kept(6, 20, 16, 128), kept(16, 16, 128), kept(16, 16, 128), kept(2, 5, 16, 128)),
         in_specs=[hbm] * 10 + [pl.BlockSpec(memory_space=pltpu.SMEM)],
-        out_specs=(on_chip, on_chip),
+        out_specs=(on_chip,) * 5,
         scratch_shapes=[
             vmem((3, 16, 16, 128), F32),
-            vmem((6, 20, 16, 128), F32),
-            vmem((16, 16, 128), F32),
-            vmem((16, 16, 128), F32),
             vmem((16, 16, 128), F32),
             vmem((1, 6, 1, 64), F32),
             vmem((1, 1, 64), F32),
@@ -460,8 +513,7 @@
             vmem((1, 1, 64), jnp.int32),
             vmem((1, 1, 64), jnp.int32),
             vmem((3, 16, 16, 128), F32),
-            vmem((3, 20, 16, 128), F32),
-            vmem((8, 3, 2, 16, 128), F32),
+            vmem((12, 3, 2, 16, 128), F32),
             vmem((4, 120, 128), F32),
             vmem((4, 120, 128), F32),
             vmem((4, 5, 16, 128), F32),
@@ -478,12 +530,12 @@
         name="elastic_step",
     )(*map(leave, args), count)
     return pl.pallas_call(
-        store,
-        out_shape=(pltpu.HBM(velocity.shape, F32), pltpu.HBM(stress.shape, F32)),
-        in_specs=[on_chip] * 2,
+        finish,
+        out_shape=(result(velocity.shape), result(stress.shape)),
+        in_specs=[on_chip] * 5,
         out_specs=(hbm, hbm),
-        scratch_shapes=[pltpu.SemaphoreType.DMA((2,))],
-        name="store_fields",
+        scratch_shapes=[vmem(stress.shape, F32), pltpu.SemaphoreType.DMA((5,))],
+        name="new_stress",
     )(*map(keep, done))
 
 

time: 29 us -> 27.7 us (0.955)
  Pallas kernels: 27.5 us -> 26.3 us
    pallas_call x2, Pallas kernels: 27.5 us -> 26.3 us  [the longest x1 25.1 us: local(): pl.pallas_call(functools.partial(kernel, nx, ny), out_shape=(kept(3, 20,...]
where the time goes in v3:
time: 27.7 us; the launch traced here: 27.5 us
  Pallas kernels  26.3 us (95%)
  between operations  1.29 us (5%)
    pallas_call x1, Pallas kernels, local(): pl.pallas_call(functools.partial(kernel, nx, ny), out_shape=(kept(3, 20,...  25.1 us
    pallas_call x1, Pallas kernels, local(): pl.pallas_call(finish, out_shape=(result(velocity.shape), result(stress.s...  1.18 us

profile of v3, /device:TPU:31, one launch (start us, length us, event | category | flops | bytes accessed | tf_op | source)
XLA Modules:
  0.0 27.5 jit_solution(16768664016363401520)
XLA Ops:
  1.3 25.1 %elastic_step.1 = (f32[3,20,16,128]{3,2,1,0:T(8,128)S(1)}, f32[6,20,16,128]{3,2,1,0:T(8,128)S(1)}, f32[16,16,128]{2,1,0:T(8,128)S(1)}, f32[16,16,128]{2,1,0:T(8,128)S(1)}, f32[2,5,16,128]{3,2,1,0:T(8,128)S(1)}) custom-call(f32[3,16,16,128]{3,2,1,0:T(8,128)} %v_in.1, f32[6,16,16,128]{3,2,1,0:T(8,128)} %s_in.1, f32[16,16,128]{2,1,0:T(8,128)} %b_in.1, ...), custom_call_target="tpu_custom_call" | custom-call | tf_op jit(solution)/shard_map/elastic_step/pallas_call | solution.py:502
  26.4 1.2 %new_stress.1 = (f32[3,16,16,128]{3,2,1,0:T(8,128)}, f32[6,16,16,128]{3,2,1,0:T(8,128)}) custom-call(f32[3,20,16,128]{3,2,1,0:T(8,128)S(1)} %get-tuple-element.7.u, f32[6,20,16,128]{3,2,1,0:T(8,128)S(1)} %get-tuple-element.8.st, f32[16,16,128]{2,1,0:T(8,128)S(1)} %get-tuple-element.9.lam, f32[16,16,128]{2,1,0:T(8,128)S(1)} %get-tuple-element.10.mu, ...), custom_call_target="tpu_custom_call" | custom-call | tf_op jit(solution)/shard_map/new_stress/pallas_call | solution.py:532

commit v4 on v3

--- a/solution.py
+++ b/solution.py
@@ -148,6 +148,42 @@
     return diff(m2, m1, f, p1)
 
 
+def stress_plane(u, st, lam, mu, edge, ns, x, rows):
+    p = x + 2
+    cells = pl.ds(rows, 8)
+
+    def low(k):
+        return edge[0, k, pl.ds(x, 1), :]
+
+    def high(k):
+        return edge[1, k, pl.ds(x, 1), :]
+
+    def part(value):
+        return value[rows : rows + 8]
+
+    ux, uy, uz = u[0, p], u[1, p], u[2, p]
+    exx = diff(u[0, p - 2, cells], u[0, p - 1, cells], part(ux), u[0, p + 1, cells])
+    eyy = part(along_y(uy, low(0), low(1), high(0), None, False))
+    ezz = along_z(part(uz), False)
+    m = mu[x, cells]
+    two = (2.0 * time_step) * m
+    press = time_step * lam[x, cells] * (exx + eyy + ezz)
+    shear = time_step * m
+    ns[0, x, cells] = st[0, p, cells] + (press + two * exx)
+    ns[1, x, cells] = st[1, p, cells] + (press + two * eyy)
+    ns[2, x, cells] = st[2, p, cells] + (press + two * ezz)
+    ns[3, x, cells] = st[3, p, cells] + shear * (
+        part(along_y(ux, None, low(2), high(1), high(2), True))
+        + diff(u[1, p - 1, cells], part(uy), u[1, p + 1, cells], u[1, p + 2, cells])
+    )
+    ns[4, x, cells] = st[4, p, cells] + shear * (
+        along_z(part(ux), True) + diff(u[2, p - 1, cells], part(uz), u[2, p + 1, cells], u[2, p + 2, cells])
+    )
+    ns[5, x, cells] = st[5, p, cells] + shear * (
+        along_z(part(uy), True) + part(along_y(uz, None, low(3), high(3), high(4), True))
+    )
+
+
 def planes(plane):
     def group(i, _):
         for k in range(4):
@@ -160,10 +196,10 @@
 def kernel(
     nx, ny,
     v_in, s_in, b_in, l_in, m_in, mom_in, sig_in, px_in, py_in, pz_in, cnt_in,
-    u, st, lam, mu, edge,
+    u, st, lam, mu, edge, ns,
     vel, buo, mom, sig, px, py, pz,
     force, forces, face_out, face_in, speed_out, speed_in, corner_out, corner_in,
-    load_sem, send_sem, recv_sem,
+    load_sem, send_sem, recv_sem, ready,
 ):
     gx, gy = lax.axis_index("gx"), lax.axis_index("gy")
 
@@ -175,19 +211,25 @@
         return ok
 
     barrier = pltpu.get_barrier_semaphore()
-    expected = 0
+    expected, expected_below = 0, 0
     for dx, dy in neighbours:
-        expected = expected + there(dx, dy).astype(jnp.int32)
-
-        @pl.when(there(dx, dy))
-        def _():
-            pl.semaphore_signal(barrier, inc=1, device_id=(gx + dx, gy + dy), device_id_type=MESH)
+        if dy >= 0:
+            expected = expected + there(dx, dy).astype(jnp.int32)
+        else:
+            expected_below = expected_below + there(dx, dy).astype(jnp.int32)
+        if dy <= 0:
+            @pl.when(there(dx, dy))
+            def _():
+                pl.semaphore_signal(barrier, inc=1, device_id=(gx + dx, gy + dy), device_id_type=MESH)
 
     loads = {}
     for k, (name, src, dst) in enumerate((
+        ("sxy", s_in.at[3, :, 8:16], st.at[3, 2:18, 8:16]), ("syy", s_in.at[1, :, 8:16], st.at[1, 2:18, 8:16]),
+        ("syz", s_in.at[5, :, 8:16], st.at[5, 2:18, 8:16]), ("buo", b_in, buo),
         ("mom", mom_in, mom), ("sig", sig_in, sig), ("px", px_in, px), ("py", py_in, py),
-        ("pz", pz_in, pz),
-        ("st", s_in, st.at[:, 2:18]), ("buo", b_in, buo), ("vel", v_in, vel),
+        ("pz", pz_in, pz), ("sxx", s_in.at[0], st.at[0, 2:18]), ("sxz", s_in.at[4], st.at[4, 2:18]),
+        ("sxy low", s_in.at[3, :, 0:8], st.at[3, 2:18, 0:8]), ("syy low", s_in.at[1, :, 0:8], st.at[1, 2:18, 0:8]),
+        ("syz low", s_in.at[5, :, 0:8], st.at[5, 2:18, 0:8]), ("szz", s_in.at[2], st.at[2, 2:18]), ("vel", v_in, vel),
         ("lam", l_in, lam), ("mu", m_in, mu),
     )):
         loads[name] = pltpu.make_async_copy(src, dst, load_sem.at[k])
@@ -211,6 +253,13 @@
         @pl.when(jnp.logical_not(there(*n)))
         def _():
             corner_in[k] = jnp.zeros((24, 128), F32)
+
+    pl.semaphore_wait(barrier, expected)
+    for dx, dy in neighbours:
+        if dy > 0:
+            @pl.when(there(dx, dy))
+            def _():
+                pl.semaphore_signal(ready, inc=1, device_id=(gx + dx, gy + dy), device_id_type=MESH)
 
     for name in ("mom", "sig", "px", "py", "pz"):
         loads[name].wait()
@@ -246,12 +295,13 @@
         size = -(-(6 + len(lists[back])) // 8) * 8
         copies["corner", back] = remote(8 + k, corner_out.at[k, 0:size], corner_in.at[3 - k, 0:size], n)
 
-    def start(kind):
-        for (what, back), copy in copies.items():
-            if what == kind:
-                @pl.when(there(-back[0], -back[1]))
-                def _():
-                    copy.start()
+    def start(kind, towards):
+        for k in towards:
+            n = (corners if kind == "corner" else sides)[k]
+
+            @pl.when(there(*n))
+            def _():
+                copies[kind, (-n[0], -n[1])].start()
 
     def arrive(kind, n):
         @pl.when(there(*n))
@@ -261,9 +311,7 @@
     def layer(ref, axis, f, at):
         return ref[f, at + 2] if axis == 0 else ref[f, 2:18, at, :]
 
-    loads["st"].wait()
-    loads["buo"].wait()
-    for k in range(4):
+    def side_message(k):
         axis, upward = k // 2, k % 2 == 1
         at = head
         for name, index in stress_of_p if upward else stress_of_q:
@@ -272,40 +320,89 @@
         for index in (14, 15) if upward else (0, 1):
             face_out[k, at : at + 16, :] = buo[index] if axis == 0 else buo[:, index, :]
             at += 16
-    for k, n in enumerate(corners):
-        for r, (f, x, y) in enumerate(lists[-n[0], -n[1]]):
+
+    def corner_message(k):
+        cells = lists[-corners[k][0], -corners[k][1]]
+        for r, (f, x, y) in enumerate(cells):
             corner_out[k, 6 + r : 7 + r, :] = st[f, 2 + x, y : y + 1, :]
-        if 6 + len(lists[-n[0], -n[1]]) > 16:
-            corner_out[k, 6 + len(lists[-n[0], -n[1]]) : 24, :] = jnp.zeros((18 - len(lists[-n[0], -n[1]]), 128), F32)
-
-    pl.semaphore_wait(barrier, expected)
-    start("face")
-    start("corner")
+        if 6 + len(cells) > 16:
+            corner_out[k, 6 + len(cells) : 24, :] = jnp.zeros((18 - len(cells), 128), F32)
+
+    for name in ("sxy", "syy", "syz", "buo"):
+        loads[name].wait()
+    side_message(3)
+    for name in ("sxx", "sxz"):
+        loads[name].wait()
+    corner_message(1)
+    corner_message(3)
+    start("corner", (1, 3))
+    start("face", (3,))
+    for name in ("sxy low", "syy low", "syz low"):
+        loads[name].wait()
+    side_message(1)
+    side_message(0)
+    start("face", (1, 0))
+    side_message(2)
+    corner_message(0)
+    corner_message(2)
 
     me = unpack(own_rows)
     force[...] = spread(me, (0, 0), [(0, tuple(range(16)), 0, 16)])[0].reshape(3, 16, 16, 128)
+
+    loads["szz"].wait()
     loads["vel"].wait()
 
-    def velocity_plane(x):
+    def velocity_plane(x, rows):
         p = x + 2
-        sxy, syy, szz, sxz, syz = st[3, p], st[1, p], st[2, p], st[4, p], st[5, p]
-        ax = diff(st[0, p - 1], st[0, p], st[0, p + 1], st[0, p + 2])
-        ax += along_y(sxy, 0.0, 0.0, 0.0, 0.0, False) + along_z(sxz, False)
-        ay = diff(st[3, p - 2], st[3, p - 1], sxy, st[3, p + 1])
-        ay += along_y(syy, 0.0, 0.0, 0.0, 0.0, True) + along_z(syz, False)
-        az = diff(st[4, p - 2], st[4, p - 1], sxz, st[4, p + 1])
-        az += along_y(syz, 0.0, 0.0, 0.0, 0.0, False) + along_z(szz, True)
-        scale = time_step * buo[x]
-        u[0, p] = vel[0, x] + scale * (ax + force[0, x])
-        u[1, p] = vel[1, x] + scale * (ay + force[1, x])
-        u[2, p] = vel[2, x] + scale * (az + force[2, x])
-
-    planes(velocity_plane)
-    for k in range(4):
+        cells = pl.ds(rows, 8)
+
+        def part(value):
+            return value[rows : rows + 8]
+
+        def share_y(f, at, forward):
+            return part(along_y(st[f, at], 0.0, 0.0, 0.0, 0.0, forward))
+
+        def share_z(f, at, forward):
+            return along_z(st[f, at, cells], forward)
+
+        ax = diff(st[0, p - 1, cells], st[0, p, cells], st[0, p + 1, cells], st[0, p + 2, cells])
+        ax += share_y(3, p, False) + share_z(4, p, False)
+        ay = diff(st[3, p - 2, cells], st[3, p - 1, cells], st[3, p, cells], st[3, p + 1, cells])
+        ay += share_y(1, p, True) + share_z(5, p, False)
+        az = diff(st[4, p - 2, cells], st[4, p - 1, cells], st[4, p, cells], st[4, p + 1, cells])
+        az += share_y(5, p, False) + share_z(2, p, True)
+        scale = time_step * buo[x, cells]
+        u[0, p, cells] = vel[0, x, cells] + scale * (ax + force[0, x, cells])
+        u[1, p, cells] = vel[1, x, cells] + scale * (ay + force[1, x, cells])
+        u[2, p, cells] = vel[2, x, cells] + scale * (az + force[2, x, cells])
+
+    def speed_message(k):
         axis, upward = k // 2, k % 2 == 1
         for at, (name, index) in enumerate(speed_of_p if upward else speed_of_q):
             speed_out[k, at] = layer(u, axis, component[axis][name], index)
-    start("speed")
+
+    planes(lambda x: velocity_plane(x, 8))
+    speed_message(3)
+    start("speed", (3,))
+    planes(lambda x: velocity_plane(x, 0))
+    for k in (1, 0, 2):
+        speed_message(k)
+    start("speed", (1, 0))
+
+    def downward():
+        @pl.when(gy > 0)
+        def _():
+            pl.semaphore_wait(ready, expected_below)
+
+        start("face", (2,))
+        start("corner", (0, 2))
+        start("speed", (2,))
+
+    patient = gy == ny // 2
+
+    @pl.when(jnp.logical_not(patient))
+    def _():
+        downward()
 
     def add_force(tile, n, pieces, shelf=None):
         parts = spread(tile, n, [piece for _, piece in pieces])
@@ -430,55 +527,39 @@
     come(early)
     for k in (3, 1, 0):
         share(k)
+    loads["lam"].wait()
+    loads["mu"].wait()
+    edge[0] = jnp.zeros((5, 16, 128), F32)
+    planes(lambda x: stress_plane(u, st, lam, mu, edge, ns, x, 8))
+
+    @pl.when(patient)
+    def _():
+        downward()
+
     come(late)
     for k in (1, 0):
         late_share(k)
     share(2)
 
-    loads["lam"].wait()
-    loads["mu"].wait()
-
     for (what, back), copy in copies.items():
         @pl.when(there(-back[0], -back[1]))
         def _():
             copy.wait_send()
 
 
-def finish(u, st, lam, mu, edge, v_out, s_out, ns, sem):
-    copies = [pltpu.make_async_copy(u.at[:, 2:18], v_out, sem.at[4])]
-    copies[0].start()
-
-    def stress_plane(x):
-        p = x + 2
-
-        def low(k):
-            return edge[0, k, x : x + 1, :]
-
-        def high(k):
-            return edge[1, k, x : x + 1, :]
-
-        ux, uy, uz = u[0, p], u[1, p], u[2, p]
-        exx = diff(u[0, p - 2], u[0, p - 1], ux, u[0, p + 1])
-        eyy = along_y(uy, low(0), low(1), high(0), None, False)
-        ezz = along_z(uz, False)
-        two = (2.0 * time_step) * mu[x]
-        press = time_step * lam[x] * (exx + eyy + ezz)
-        shear = time_step * mu[x]
-        ns[0, x] = st[0, p] + (press + two * exx)
-        ns[1, x] = st[1, p] + (press + two * eyy)
-        ns[2, x] = st[2, p] + (press + two * ezz)
-        ns[3, x] = st[3, p] + shear * (
-            along_y(ux, None, low(2), high(1), high(2), True)
-            + diff(u[1, p - 1], uy, u[1, p + 1], u[1, p + 2])
-        )
-        ns[4, x] = st[4, p] + shear * (along_z(ux, True) + diff(u[2, p - 1], uz, u[2, p + 1], u[2, p + 2]))
-        ns[5, x] = st[5, p] + shear * (along_z(uy, True) + along_y(uz, None, low(3), high(3), high(4), True))
+def finish(u, st, lam, mu, edge, high, v_out, s_out, low, sem):
+    copies = [
+        pltpu.make_async_copy(u.at[:, 2:18], v_out, sem.at[4]),
+        pltpu.make_async_copy(high.at[:, :, 8:16], s_out.at[:, :, 8:16], sem.at[5]),
+    ]
+    for copy in copies:
+        copy.start()
 
     for part in range(4):
         cells = pl.ds(4 * part, 4)
         for x in range(4 * part, 4 * part + 4):
-            stress_plane(x)
-        copies.append(pltpu.make_async_copy(ns.at[:, cells], s_out.at[:, cells], sem.at[part]))
+            stress_plane(u, st, lam, mu, edge, low, x, 0)
+        copies.append(pltpu.make_async_copy(low.at[:, cells], s_out.at[:, cells, 0:8], sem.at[part]))
         copies[-1].start()
     for copy in copies:
         copy.wait()
@@ -501,9 +582,9 @@
     args = (velocity, stress, buoyancy, lame_lambda, shear_modulus, jnp.transpose(moment, (0, 2, 1, 3)), signal, sx, sy, sz)
     done = pl.pallas_call(
         functools.partial(kernel, nx, ny),
-        out_shape=(kept(3, 20, 16, 128), kept(6, 20, 16, 128), kept(16, 16, 128), kept(16, 16, 128), kept(2, 5, 16, 128)),
+        out_shape=(kept(3, 20, 16, 128), kept(6, 20, 16, 128), kept(16, 16, 128), kept(16, 16, 128), kept(2, 5, 16, 128), kept(6, 16, 16, 128)),
         in_specs=[hbm] * 10 + [pl.BlockSpec(memory_space=pltpu.SMEM)],
-        out_specs=(on_chip,) * 5,
+        out_specs=(on_chip,) * 6,
         scratch_shapes=[
             vmem((3, 16, 16, 128), F32),
             vmem((16, 16, 128), F32),
@@ -520,9 +601,10 @@
             vmem((4, 5, 16, 128), F32),
             vmem((4, 24, 128), F32),
             vmem((4, 24, 128), F32),
-            pltpu.SemaphoreType.DMA((10,)),
+            pltpu.SemaphoreType.DMA((18,)),
             pltpu.SemaphoreType.DMA((12,)),
             pltpu.SemaphoreType.DMA((12,)),
+            pltpu.SemaphoreType.REGULAR,
         ],
         compiler_params=pltpu.CompilerParams(
             collective_id=0, has_side_effects=True, vmem_limit_bytes=48 * 1024 * 1024
@@ -532,9 +614,9 @@
     return pl.pallas_call(
         finish,
         out_shape=(result(velocity.shape), result(stress.shape)),
-        in_specs=[on_chip] * 5,
+        in_specs=[on_chip] * 6,
         out_specs=(hbm, hbm),
-        scratch_shapes=[vmem(stress.shape, F32), pltpu.SemaphoreType.DMA((5,))],
+        scratch_shapes=[vmem((6, 16, 8, 128), F32), pltpu.SemaphoreType.DMA((6,))],
         name="new_stress",
     )(*map(keep, done))
 

time: 27.7 us -> 26.9 us (0.971)
  the two profiles are of different devices: /device:TPU:31 before, /device:TPU:6 now
where the time goes in v4:
time: 26.9 us; the launch traced here: 26.7 us
  Pallas kernels  25.4 us (94%)
  between operations  1.29 us (5%)
    pallas_call x1, Pallas kernels, local(): pl.pallas_call(functools.partial(kernel, nx, ny), out_shape=(kept(3, 20,...  24.3 us
    pallas_call x1, Pallas kernels, local(): pl.pallas_call(finish, out_shape=(result(velocity.shape), result(stress.s...  1.14 us

profile of v4, /device:TPU:6, one launch (start us, length us, event | category | flops | bytes accessed | tf_op | source)
XLA Modules:
  0.0 26.7 jit_solution(4234987418188814358)
XLA Ops:
  1.3 24.3 %elastic_step.1 = (f32[3,20,16,128]{3,2,1,0:T(8,128)S(1)}, f32[6,20,16,128]{3,2,1,0:T(8,128)S(1)}, f32[16,16,128]{2,1,0:T(8,128)S(1)}, f32[16,16,128]{2,1,0:T(8,...) custom-call(f32[3,16,16,128]{3,2,1,0:T(8,128)} %v_in.1, f32[6,16,16,128]{3,2,1,0:T(8,128)} %s_in.1, ...), custom_call_target="tpu_custom_call" | custom-call | tf_op jit(solution)/shard_map/elastic_step/pallas_call | solution.py:583
  25.6 1.1 %new_stress.1 = (f32[3,16,16,128]{3,2,1,0:T(8,128)}, f32[6,16,16,128]{3,2,1,0:T(8,128)}) custom-call(f32[3,20,16,128]{3,2,1,0:T(8,128)S(1)} %get-tuple-element.8.u, f32[6,20,16,128]{3,2,1,0:T(8,128)S(1)} %get-tuple-element.9.st, f32[16,16,128]{2,1,0:T(8,128)S(1)} %get-tuple-element.10.lam, f32[16,16,128]{2,1,0:T(8,128)S(1)} %get-tuple-element.11.mu, ...), custom_call_target="tpu_custom_call" | custom-call | tf_op jit(solution)/shard_map/new_stress/pallas_call | solution.py:614

commit v5 on v4

--- a/solution.py
+++ b/solution.py
@@ -225,9 +225,10 @@
     loads = {}
     for k, (name, src, dst) in enumerate((
         ("sxy", s_in.at[3, :, 8:16], st.at[3, 2:18, 8:16]), ("syy", s_in.at[1, :, 8:16], st.at[1, 2:18, 8:16]),
-        ("syz", s_in.at[5, :, 8:16], st.at[5, 2:18, 8:16]), ("buo", b_in, buo),
+        ("syz", s_in.at[5, :, 8:16], st.at[5, 2:18, 8:16]),
         ("mom", mom_in, mom), ("sig", sig_in, sig), ("px", px_in, px), ("py", py_in, py),
         ("pz", pz_in, pz), ("sxx", s_in.at[0], st.at[0, 2:18]), ("sxz", s_in.at[4], st.at[4, 2:18]),
+        ("buo", b_in, buo),
         ("sxy low", s_in.at[3, :, 0:8], st.at[3, 2:18, 0:8]), ("syy low", s_in.at[1, :, 0:8], st.at[1, 2:18, 0:8]),
         ("syz low", s_in.at[5, :, 0:8], st.at[5, 2:18, 0:8]), ("szz", s_in.at[2], st.at[2, 2:18]), ("vel", v_in, vel),
         ("lam", l_in, lam), ("mu", m_in, mu),
@@ -246,8 +247,8 @@
     for k, n in enumerate(sides):
         @pl.when(jnp.logical_not(there(*n)))
         def _():
-            face_in[k] = jnp.zeros((120, 128), F32)
-            speed_in[k] = jnp.zeros((5, 16, 128), F32)
+            face_in[k] = jnp.zeros((88, 128), F32)
+            speed_in[k] = jnp.zeros((7, 16, 128), F32)
 
     for k, n in enumerate(corners):
         @pl.when(jnp.logical_not(there(*n)))
@@ -285,8 +286,8 @@
     copies = {}
     for k, n in enumerate(sides):
         upward = k % 2 == 1
-        size = head + 16 * (len(stress_of_p if upward else stress_of_q) + 2)
-        count = len(speed_of_p if upward else speed_of_q)
+        size = head + 16 * len(stress_of_p if upward else stress_of_q)
+        count = len(speed_of_p if upward else speed_of_q) + 2
         back = (-n[0], -n[1])
         copies["face", back] = remote(k, face_out.at[k, 0:size], face_in.at[k ^ 1, 0:size], n)
         copies["speed", back] = remote(4 + k, speed_out.at[k, 0:count], speed_in.at[k ^ 1, 0:count], n)
@@ -317,9 +318,6 @@
         for name, index in stress_of_p if upward else stress_of_q:
             face_out[k, at : at + 16, :] = layer(st, axis, field[axis][name], index)
             at += 16
-        for index in (14, 15) if upward else (0, 1):
-            face_out[k, at : at + 16, :] = buo[index] if axis == 0 else buo[:, index, :]
-            at += 16
 
     def corner_message(k):
         cells = lists[-corners[k][0], -corners[k][1]]
@@ -328,7 +326,7 @@
         if 6 + len(cells) > 16:
             corner_out[k, 6 + len(cells) : 24, :] = jnp.zeros((18 - len(cells), 128), F32)
 
-    for name in ("sxy", "syy", "syz", "buo"):
+    for name in ("sxy", "syy", "syz"):
         loads[name].wait()
     side_message(3)
     for name in ("sxx", "sxz"):
@@ -350,6 +348,7 @@
     force[...] = spread(me, (0, 0), [(0, tuple(range(16)), 0, 16)])[0].reshape(3, 16, 16, 128)
 
     loads["szz"].wait()
+    loads["buo"].wait()
     loads["vel"].wait()
 
     def velocity_plane(x, rows):
@@ -380,6 +379,8 @@
         axis, upward = k // 2, k % 2 == 1
         for at, (name, index) in enumerate(speed_of_p if upward else speed_of_q):
             speed_out[k, at] = layer(u, axis, component[axis][name], index)
+        for at, index in enumerate((14, 15) if upward else (0, 1), at + 1):
+            speed_out[k, at] = buo[index] if axis == 0 else buo[:, index, :]
 
     planes(lambda x: velocity_plane(x, 8))
     speed_message(3)
@@ -502,8 +503,8 @@
             for along in (1,) if axis == 0 else (-1, 1):
                 for where, value in corner_share(k, name, index, along):
                     acc = acc + jnp.where(row == where, value, 0.0)
-            b_at = head + 16 * (len(layers) + near)
-            total = speed_in[k, at] + time_step * face_in[k, b_at : b_at + 16, :] * acc
+            b_at = len(speed_of_q if upward else speed_of_p) + near
+            total = speed_in[k, at] + time_step * speed_in[k, b_at] * acc
             if axis == 0:
                 u[c, (18 if upward else 0) + near] = total
             else:
@@ -521,8 +522,8 @@
             acc = forces[shelf[4 + k], c, near, 0:8, :]
             for where, value in corner_share(k, name, index, -1):
                 acc = acc + jnp.where(row[0:8] == where, value, 0.0)
-            b_at = head + 16 * (len(stress_of_q if upward else stress_of_p) + near)
-            u[c, (18 if upward else 0) + near, 0:8, :] += time_step * face_in[k, b_at : b_at + 8, :] * acc
+            b_at = len(speed_of_q if upward else speed_of_p) + near
+            u[c, (18 if upward else 0) + near, 0:8, :] += time_step * speed_in[k, b_at, 0:8, :] * acc
 
     come(early)
     for k in (3, 1, 0):
@@ -595,10 +596,10 @@
             vmem((1, 1, 64), jnp.int32),
             vmem((3, 16, 16, 128), F32),
             vmem((12, 3, 2, 16, 128), F32),
-            vmem((4, 120, 128), F32),
-            vmem((4, 120, 128), F32),
-            vmem((4, 5, 16, 128), F32),
-            vmem((4, 5, 16, 128), F32),
+            vmem((4, 88, 128), F32),
+            vmem((4, 88, 128), F32),
+            vmem((4, 7, 16, 128), F32),
+            vmem((4, 7, 16, 128), F32),
             vmem((4, 24, 128), F32),
             vmem((4, 24, 128), F32),
             pltpu.SemaphoreType.DMA((18,)),

time: 26.9 us -> 27 us (level)
  no operation moved by 1% of the time
where the time goes in v5:
time: 27 us; the launch traced here: 26.8 us
  Pallas kernels  25.6 us (95%)
  between operations  1.29 us (5%)
    pallas_call x1, Pallas kernels, local(): pl.pallas_call(functools.partial(kernel, nx, ny), out_shape=(kept(3, 20,...  24.4 us
    pallas_call x1, Pallas kernels, local(): pl.pallas_call(finish, out_shape=(result(velocity.shape), result(stress.s...  1.14 us

profile of v5, /device:TPU:6, one launch (start us, length us, event | category | flops | bytes accessed | tf_op | source)
XLA Modules:
  0.0 26.8 jit_solution(3537594700194420723)
XLA Ops:
  1.3 24.4 %elastic_step.1 = (f32[3,20,16,128]{3,2,1,0:T(8,128)S(1)}, f32[6,20,16,128]{3,2,1,0:T(8,128)S(1)}, f32[16,16,128]{2,1,0:T(8,128)S(1)}, f32[16,16,128]{2,1,0:T(8,...) custom-call(f32[3,16,16,128]{3,2,1,0:T(8,128)} %v_in.1, f32[6,16,16,128]{3,2,1,0:T(8,128)} %s_in.1, ...), custom_call_target="tpu_custom_call" | custom-call | tf_op jit(solution)/shard_map/elastic_step/pallas_call | solution.py:584
  25.7 1.1 %new_stress.1 = (f32[3,16,16,128]{3,2,1,0:T(8,128)}, f32[6,16,16,128]{3,2,1,0:T(8,128)}) custom-call(f32[3,20,16,128]{3,2,1,0:T(8,128)S(1)} %get-tuple-element.8.u, f32[6,20,16,128]{3,2,1,0:T(8,128)S(1)} %get-tuple-element.9.st, f32[16,16,128]{2,1,0:T(8,128)S(1)} %get-tuple-element.10.lam, f32[16,16,128]{2,1,0:T(8,128)S(1)} %get-tuple-element.11.mu, ...), custom_call_target="tpu_custom_call" | custom-call | tf_op jit(solution)/shard_map/new_stress/pallas_call | solution.py:615
